TPU v7x, 256 devices: a whole 4x4x8 slice. The times are simulated.
256 devices in a mesh: dp: 8 (over z), expert: 32 (over x, y, core).
Axes of the slice: x: 4, y: 4, z: 8, core: 2. Of those that a mesh axis runs over, the one named last changes fastest.
Arguments:
- grad_out: bfloat16 [32768, 4096], P(('dp', 'expert')), may hold values from -6 to 6
- expert_ids: int32 [32768, 8], P(('dp', 'expert')), may hold values from 0 to 63, all different within a row; in each aligned block of 128 rows (0 to 127, 128 to 255, ...) at most 17 rows name the same one
- gate_weights: bfloat16 [32768, 8], P(('dp', 'expert')), may hold values from 0.019897461 to 0.5
- saved_gate: bfloat16 [64, 4352, 768], P('expert', 'dp'), may hold values from -6 to 6
- saved_up: bfloat16 [64, 4352, 768], P('expert', 'dp'), may hold values from -6 to 6
- down_weight: bfloat16 [768, 64, 4096], P('dp', 'expert'), may hold values from -0.21875 to 0.21875
Outputs:
- grad_gate: bfloat16 [64, 4352, 768], P('expert', 'dp')
- grad_up: bfloat16 [64, 4352, 768], P('expert', 'dp')
- grad_down: float32 [768, 64, 4096], P('dp', 'expert')
Inputs may be any that keep to these rules, and one draw needn't show every extreme that they name: `expert_ids`: among the tokens of one device (aligned blocks of 128 rows) no expert is named more than 17 times, a bound that some block reaches; a token names 8 different experts.
All inputs are finite; a program needn't handle non-finite values.
Results may differ from a plain program's by a relative error of at most 0.015.
Values may be sent and summed in bfloat16 or wider, within the bound.
No kernel may reach another device: no remote copies, remote signals or barrier semaphores. Data moves between devices by JAX's collectives and lax.ppermute only.
A program may use at most 192 MiB of HBM per device.

v0:
```python
import jax
import jax.numpy as jnp
from jax import lax
from jax.sharding import PartitionSpec as P


def on_device(grad_out, expert_ids, gate_weights, saved_gate, saved_up, down_weight):
    token_count = grad_out.shape[0]
    width = grad_out.shape[1]
    top_count = expert_ids.shape[1]
    local_experts = down_weight.shape[1]
    sources = lax.axis_size("expert")
    experts = local_experts * sources
    capacity = saved_gate.shape[1] // sources
    flat_ids = expert_ids.reshape(token_count * top_count)
    onehot = (flat_ids[:, None] == jnp.arange(experts, dtype=jnp.int32)[None, :]).astype(jnp.int32)
    slot_rank = jnp.sum((jnp.cumsum(onehot, axis=0) - onehot) * onehot, axis=1)
    repeated = jnp.broadcast_to(grad_out[:, None, :], (token_count, top_count, width)).reshape(
        token_count * top_count, width
    )
    row_buffer = (
        jnp.zeros((experts, capacity, width), jnp.bfloat16).at[flat_ids, slot_rank].set(repeated)
    )
    gate_buffer = (
        jnp.zeros((experts, capacity), jnp.bfloat16)
        .at[flat_ids, slot_rank]
        .set(gate_weights.reshape(token_count * top_count))
    )
    arrived_rows, arrived_gates = (
        lax.all_to_all(row_buffer, "expert", split_axis=0, concat_axis=1, tiled=True),
        lax.all_to_all(gate_buffer, "expert", split_axis=0, concat_axis=1, tiled=True),
    )
    dispatched = (
        arrived_gates[:, :, None].astype(jnp.float32) * arrived_rows.astype(jnp.float32)
    ).astype(jnp.bfloat16)
    gate_f = saved_gate.astype(jnp.float32)
    up_f = saved_up.astype(jnp.float32)
    logistic = jax.nn.sigmoid(gate_f)
    activated = gate_f * logistic
    hidden = (activated * up_f).astype(jnp.bfloat16)
    grad_hidden = jnp.einsum(
        "esd,fed->esf",
        dispatched,
        lax.all_gather(down_weight, "dp", axis=0, tiled=True),
        preferred_element_type=jnp.float32,
    )
    grad_gate = (grad_hidden * up_f * logistic * (1.0 + gate_f * (1.0 - logistic))).astype(
        jnp.bfloat16
    )
    grad_up = (grad_hidden * activated).astype(jnp.bfloat16)
    grad_down = lax.psum_scatter(
        jnp.einsum("esf,esd->fed", hidden, dispatched, preferred_element_type=jnp.float32).astype(
            jnp.bfloat16
        ),
        "dp",
        scatter_dimension=0,
        tiled=True,
    ).astype(jnp.float32)
    return (grad_gate, grad_up, grad_down)


def solution(mesh):
    in_specs = (
        P(("dp", "expert"), None),
        P(("dp", "expert"), None),
        P(("dp", "expert"), None),
        P("expert", "dp", None),
        P("expert", "dp", None),
        P("dp", "expert", None),
    )
    out_specs = (P("expert", "dp", None), P("expert", "dp", None), P("dp", "expert", None))
    return jax.shard_map(
        on_device, mesh=mesh, in_specs=in_specs, out_specs=out_specs, check_vma=False
    )
```

profile of v0, /device:TPU:8, one launch (start us, length us, event | category | flops | bytes accessed | tf_op | source)
XLA Modules:
  0.0 828.4 jit_solution(8023610959949325552)
XLA Ops:
  7.2 0.0 copy-start
  7.2 0.9 copy.69
  8.1 0.1 eq.29
  8.1 0.1 eq.25
  8.2 0.1 reshape.91
  8.4 18.0 %reduce-window.6 = s32[64,8,128]{2,1,0:T(8,128)S(1)} reduce-window(s32[64,8,128]{2,1,0:T(8,128)S(1)} %fusion.20, s32[]{:T(128)} %constant.6.clone.1), window={size=1x1x128 pad=0_0x0_0x127_0}, to_apply=%region_0.0 | reduce-window | flops 8323072 | bytes 524292 | tf_op jit(solution)/shard_map/reduce-window
  26.4 0.1 slice.8
  26.5 0.1 copy.72
  26.7 0.1 copy.73
  26.8 0.1 broadcast_add_fusion
  26.9 0.1 fusion.19
  27.0 0.7 multiply_reduce_fusion
  27.8 0.8 and_reduce_fusion
  28.5 0.8 copy.74
  29.3 0.1 reshape.108
  29.4 7.6 scatter_custom_fusion
  37.0 0.1 reshape.97
  37.1 0.7 copy.75
  37.8 7.9 all-to-all-start
  45.8 0.0 copy-done
  45.8 16.2 %scatter_custom_fusion.1 = bf16[1088,4096]{1,0:T(8,128)(2,1)} fusion(s32[1024]{0:T(1024)S(1)} %broadcast_select_fusion, bf16[]{:T(256)} %constant.5.clone.1, bf16[128,4096]{1,0:T(8,128)(2,1)S(1)} %copy-done), kind=kCustom, calls=%fused_computation.6 | custom fusion | bytes 9961474
  62.0 10.8 %copy.77 = bf16[64,17,4096]{2,1,0:T(8,128)(2,1)} copy(bf16[64,17,4096]{2,0,1:T(8,128)(2,1)} %bitcast.38) | data formatting | bytes 17825792 | tf_op jit(solution)/shard_map/scatter | solution.py:22
  72.8 0.0 all-to-all-done
  72.8 7.4 all-to-all-start.1
  80.2 0.6 all-reduce.3.cloned.1.call-start
  80.8 0.1 reshape.103
  81.0 196.7 %all-to-all-done.1 = bf16[64,17,4096]{2,1,0:T(8,128)(2,1)} async-done(((bf16[64,17,4096]{2,1,0:T(8,128)(2,1)}), bf16[64,17,4096]{2,1,0:T(8,128)(2,1)}, u32[]{:S(2)}, u32[]{:S(2)}) %all-to-all-start.1) | async-done | bytes 8912928 | tf_op jit(solution)/shard_map/all_to_all | solution.py:30
  277.6 16.2 %copy_convert_fusion = f32[64,17,4096]{2,0,1:T(8,128)} fusion(bf16[64,17,4096]{2,1,0:T(8,128)(2,1)} %all-to-all-done.1), kind=kLoop, calls=%fused_computation.5 | loop fusion | flops 4456448 | bytes 26738688 | tf_op jit(solution)/shard_map/convert_element_type | solution.py:34
  293.8 21.8 %reshape.105 = f32[32,2,17,4096]{3,1,0,2:T(2,128)} reshape(f32[64,17,4096]{2,0,1:T(8,128)} %copy_convert_fusion) | data formatting | bytes 35651584 | tf_op jit(solution)/shard_map/convert_element_type | solution.py:34
  315.6 12.7 %copy.79 = f32[2,32,17,4096]{3,0,2,1:T(2,128)} copy(f32[2,32,17,4096]{3,0,1,2:T(2,128)} %bitcast.37) | data formatting | bytes 35651584 | tf_op jit(solution)/shard_map/convert_element_type | solution.py:34
  328.3 28.8 %convert_bitcast_fusion = bf16[768,2,4096]{0,2,1:T(8,128)(2,1)} fusion(f32[2,544,4096]{2,0,1:T(2,128)} %bitcast.39, f32[2,544]{1,0:T(2,128)S(1)} %reshape.103, bf16[2,544,768]{2,1,0:T(8,128)(2,1)} %param.10, bf16[2,544,768]{2,1,0:T(8,128)(2,1)} %param.9), kind=kOutput, calls=%fused_computation.4 | convolution fusion | flops 6866993152 | bytes 33755392 | tf_op jit(solution)/shard_map/esf,esd->fed/dot_general | solution.py:52
  357.1 31.7 %copy.82 = bf16[768,2,4096]{2,1,0:T(2,128)(2,1)} copy(bf16[768,2,4096]{0,2,1:T(8,128)(2,1)} %convert_bitcast_fusion) | data formatting | bytes 25165824 | tf_op jit(solution)/shard_map/convert_element_type | solution.py:52
  388.8 0.0 copy-start.2
  388.8 0.0 all-reduce.3.cloned.1.call-update
  388.8 0.0 copy-start.3
  388.8 0.3 all-gather.2.cloned.1.call-start
  389.1 1.1 copy-done.2
  390.2 2.0 copy.81
  392.2 0.0 all-gather.2.cloned.1.call-update
  392.2 0.0 copy-done.3
  392.2 0.6 dynamic-slice
  393.5 264.9 %all-reduce.3.cloned.1.call-done = bf16[768,2,4096]{2,1,0:T(2,128)(2,1)} async-done(((bf16[768,2,4096]{2,1,0:T(2,128)(2,1)}), bf16[768,2,4096]{2,1,0:T(2,128)(2,1)}) %all-reduce.3.cloned.1.call-update) | async-done | bytes 12582928
  658.4 4.5 dynamic-slice_convert_fusion
  662.9 130.2 %all-gather.2.cloned.1.call-done = bf16[768,2,4096]{2,0,1:T(8,128)(2,1)} async-done(((bf16[96,2,4096]{2,0,1:T(8,128)(2,1)}), bf16[768,2,4096]{2,0,1:T(8,128)(2,1)}) %all-gather.2.cloned.1.call-update) | async-done | bytes 12582928 | tf_op jit(solution)/shard_map/all_gather | solution.py:44
  793.0 0.0 copy-start.1
  793.0 28.2 %multiply_convert_fusion = (bf16[2,544,768]{2,1,0:T(8,128)(2,1)}, bf16[2,544,768]{2,1,0:T(8,128)(2,1)}) fusion(bf16[2,544,768]{2,1,0:T(8,128)(2,1)} %param.9, bf16[2,544,768]{2,1,0:T(8,128)(2,1)} %param.10, bf16[768,2,4096]{2,0,1:T(8,128)(2,1)} %all-gather.2.cloned.1.call-done, f32[2,544,4096]{2,0,1:T(2,128)} %bitcast.40, f32[2,544]{1,0:T(2,128)S(1)} %reshape.103), kind=kOutput, calls=%fused_computation.23 | convolution fusion | flops 6866550784 | bytes 37097728 | tf_op jit(solution)/shard_map/esd,fed->esf/dot_general | solution.py:41
  821.3 0.0 copy-done.1
  (7 shorter events, 0.1 us)
Async XLA Ops:
  7.2 38.6 %copy-start = (bf16[128,4096]{1,0:T(8,128)(2,1)S(1)}, bf16[128,4096]{1,0:T(8,128)(2,1)}, u32[]{:S(2)}) copy-start(bf16[128,4096]{1,0:T(8,128)(2,1)} %param.6) | copy-start | bytes 3145732
  37.8 35.0 %all-to-all-start = ((bf16[32,2,17]{2,1,0:T(2,128)(2,1)}), bf16[32,2,17]{2,1,0:T(2,128)(2,1)S(1)}, u32[]{:S(2)}, u32[]{:S(2)}) async-start(bf16[32,2,17]{2,1,0:T(2,128)(2,1)} %bitcast.4), calls=%async_computation | async-start | bytes 32768 | tf_op jit(solution)/shard_map/all_to_all | solution.py:31
  72.8 204.8 %all-to-all-start.1 = ((bf16[64,17,4096]{2,1,0:T(8,128)(2,1)}), bf16[64,17,4096]{2,1,0:T(8,128)(2,1)}, u32[]{:S(2)}, u32[]{:S(2)}) async-start(bf16[64,17,4096]{2,1,0:T(8,128)(2,1)} %copy.77), calls=%async_computation.1 | async-start | bytes 25165824 | tf_op jit(solution)/shard_map/all_to_all | solution.py:30
  80.2 578.1 %all-reduce.3.cloned.1.call-start = ((), (), s32[]{:S(2)}) async-start(), calls=%async_computation.3 | async-start | bytes 25165824
  388.8 1.4 copy-start.2
  388.8 3.4 copy-start.3
  388.8 404.2 %all-gather.2.cloned.1.call-start = ((), (), s32[]{:S(2)}) async-start(), calls=%async_computation.2 | async-start | bytes 14155776 | tf_op jit(solution)/shard_map/all_gather | solution.py:44
  793.0 28.2 %copy-start.1 = (bf16[128,4096]{1,0:T(8,128)(2,1)S(1)}, bf16[128,4096]{1,0:T(8,128)(2,1)}, u32[]{:S(2)}) copy-start(bf16[128,4096]{1,0:T(8,128)(2,1)} %param.6) | copy-start | bytes 3145732
Sparse Core Ops, SparseCore 0:
  388.9 269.4 all-reduce.2
  660.8 132.2 all-gather.1
where the time goes:
time: 835 us; the launch traced here: 828 us
  waiting for transfers between devices  592 us (71%)
  local copies, waits for them, and re-layouts  108 us (13%)
  matrix products  57 us (7%)
  other arithmetic  40.5 us (5%)
  starting transfers between devices  16.2 us (2%)
  between operations  15.1 us (2%)
    unnamed x3, waiting for transfers between devices  265 us
    all_to_all x1, waiting for transfers between devices, on_device(): lax.all_to_all(row_buffer, 'expert', split_axis=0, concat_axis=1, tiled=T...  197 us
    all_gather x1, waiting for transfers between devices, on_device(): lax.all_gather(down_weight, 'dp', axis=0, tiled=True)  130 us
    convert_element_type x2, local copies, waits for them, and re-layouts, on_device(): arrived_rows.astype(jnp.float32)  34.5 us
    convert_element_type x1, local copies, waits for them, and re-layouts, on_device(): jnp.einsum('esf,esd->fed', hidden, dispatched, preferred_element_type=jnp...  31.7 us
    unnamed x15, local copies, waits for them, and re-layouts  29.3 us
    dot_general x1, matrix products, on_device(): jnp.einsum('esf,esd->fed', hidden, dispatched, preferred_element_type=jnp...  28.8 us
    dot_general x1, matrix products, on_device(): jnp.einsum('esd,fed->esf', dispatched, lax.all_gather(down_weight, 'dp',...  28.2 us
  transfers between devices with their start and end apart: 4, of which 3 were waited for; matrix products, arithmetic and copies ran while one was open for 4% of the time, Pallas kernels for 0%

commit v1 on v0

v1 whole, which is shorter than its diff:
```python
import functools

import jax
import jax.numpy as jnp
from jax import lax
from jax.experimental import pallas as pl
from jax.experimental.pallas import tpu as pltpu
from jax.sharding import PartitionSpec as P

BF = jnp.bfloat16
F32 = jnp.float32
LANE = 128
MAIN = 16
FOLD = 8
PARAMS = pltpu.CompilerParams(vmem_limit_bytes=56 * 1024 * 1024)


def dot(a, b, dims=((1,), (0,))):
    return lax.dot_general(a, b, (dims, ((), ())), preferred_element_type=F32)


def iota(shape, dim):
    return lax.broadcasted_iota(jnp.int32, shape, dim)


def dispatch_kernel(ids_ref, gates_ref, grad_ref, out_ref, main_ref, tail_ref):
    step = pl.program_id(0)
    tokens, top = ids_ref.shape
    dests = out_ref.shape[0]
    experts = 2 * dests

    @pl.when(step == 0)
    def _():
        lanes = iota((tokens, LANE), 1)
        member = jnp.zeros((tokens, LANE), F32)
        gate = jnp.zeros((tokens, LANE), F32)
        for k in range(top):
            hit = ids_ref[:, k : k + 1] == lanes
            member = member + jnp.where(hit, 1.0, 0.0)
            gate = gate + jnp.where(hit, gates_ref[:, k : k + 1].astype(F32), 0.0)
        earlier = jnp.where(iota((tokens, tokens), 1) < iota((tokens, tokens), 0), 1.0, 0.0)
        rank = dot(earlier.astype(BF), member.astype(BF))
        rank = jnp.where(member > 0.0, rank, -1.0)
        rank_t = jnp.transpose(rank)[:experts]
        gate_t = jnp.transpose(gate)[:experts]
        slots = iota((experts, MAIN, tokens), 1).astype(F32)
        chosen = jnp.where(rank_t[:, None, :] == slots, gate_t[:, None, :], 0.0)
        main_ref[...] = chosen.reshape(experts * MAIN, tokens).astype(BF)
        last = jnp.where(rank_t == float(MAIN), gate_t, 0.0)
        last = jnp.broadcast_to(last[:, None, :], (experts, FOLD, tokens)).reshape(experts * FOLD, tokens)
        rows = iota((experts * FOLD, tokens), 0) % FOLD
        for k in range(FOLD):
            tail_ref[:, k * tokens : (k + 1) * tokens] = jnp.where(rows == k, last, 0.0).astype(BF)

    @pl.when(step < pl.num_programs(0) - 1)
    def _():
        columns = grad_ref[:, pl.ds(pl.multiple_of(step * 256, 256), 256)]
        rows = dot(main_ref[...], columns).astype(BF)
        for k in range(2):
            out_ref[:, k * 32 : (k + 1) * 32, :] = rows[:, k * LANE : (k + 1) * LANE].reshape(dests, 32, LANE)

    @pl.when(step == pl.num_programs(0) - 1)
    def _():
        width = grad_ref.shape[1] // FOLD
        stacked = jnp.concatenate([grad_ref[:, k * width : (k + 1) * width] for k in range(FOLD)], axis=0)
        rows = dot(tail_ref[...], stacked).astype(BF)
        for k in range(width // LANE):
            out_ref[:, k * 16 : (k + 1) * 16, :] = rows[:, k * LANE : (k + 1) * LANE].reshape(dests, 16, LANE)


def dispatch(ids, gates, grad, dests):
    tokens, width = grad.shape
    rows = 34 * width // LANE
    steps = rows // 64
    return pl.pallas_call(
        dispatch_kernel,
        grid=(steps,),
        in_specs=[
            pl.BlockSpec(ids.shape, lambda i: (0, 0)),
            pl.BlockSpec(gates.shape, lambda i: (0, 0)),
            pl.BlockSpec(grad.shape, lambda i: (0, 0)),
        ],
        out_specs=pl.BlockSpec((dests, 64, LANE), lambda i: (0, i, 0)),
        out_shape=jax.ShapeDtypeStruct((dests, rows, LANE), BF),
        scratch_shapes=[
            pltpu.VMEM((2 * dests * MAIN, tokens), BF),
            pltpu.VMEM((2 * dests * FOLD, FOLD * tokens), BF),
        ],
        compiler_params=PARAMS,
        cost_estimate=pl.CostEstimate(flops=2 * 1088 * 128 * 4096, bytes_accessed=10 << 20, transcendentals=0),
        name="dispatch",
    )(ids, gates, grad)


def natural(order, sources):
    main = sources * MAIN
    return jnp.where(order < main, (order // MAIN) * (MAIN + 1) + order % MAIN, (order - main) * (MAIN + 1) + MAIN)


def hidden_kernel(sources, gate_ref, up_ref, out_ref):
    gate = gate_ref[0].astype(F32)
    slots = gate.shape[0]
    hidden = (gate * jax.nn.sigmoid(gate) * up_ref[0].astype(F32)).astype(BF)
    place = natural(iota((slots, slots), 1), sources) == iota((slots, slots), 0)
    place = jnp.where(place, 1.0, 0.0).astype(BF)
    out_ref[0] = dot(hidden, place, ((0,), (0,))).astype(BF)


def arranged_hidden(gate, up, sources):
    local, slots, units = gate.shape
    spec = pl.BlockSpec((1, slots, units), lambda e: (e, 0, 0))
    return pl.pallas_call(
        functools.partial(hidden_kernel, sources),
        grid=(local,),
        in_specs=[spec, spec],
        out_specs=pl.BlockSpec((1, units, slots), lambda e: (e, 0, 0)),
        out_shape=jax.ShapeDtypeStruct((local, units, slots), BF),
        compiler_params=PARAMS,
        cost_estimate=pl.CostEstimate(flops=4 * slots * slots * units, bytes_accessed=6 << 20, transcendentals=local * slots * units),
        name="hidden",
    )(gate, up)


def unfold(tail_ref, out_ref):
    sources = tail_ref.shape[0]
    rows = sources * 16
    folded = jnp.concatenate([tail_ref[:, k * 16 : (k + 1) * 16, :].reshape(rows, LANE) for k in range(4)], axis=1)
    row = iota((2 * sources, rows), 0)
    column = iota((2 * sources, rows), 1)
    for k in range(FOLD):
        pick = column == (row % sources) * 16 + (row // sources) * FOLD + k
        out_ref[k] = dot(jnp.where(pick, 1.0, 0.0).astype(BF), folded).astype(BF)


def expert_rows(rows_ref, expert):
    sources = rows_ref.shape[0]
    return jnp.concatenate(
        [
            rows_ref[:, k * 32 + expert * 16 : k * 32 + expert * 16 + 16, :].reshape(sources * 16, LANE)
            for k in range(4)
        ],
        axis=1,
    )


def down_kernel(rows_ref, tail_ref, hidden_ref, out_ref, last_ref):
    step = pl.program_id(0)
    sources = rows_ref.shape[0]

    @pl.when(step == 0)
    def _():
        unfold(tail_ref, last_ref)

    groups, _, units, width = out_ref.shape
    main = sources * MAIN
    for e in range(2):
        total = dot(hidden_ref[e][:, :main], expert_rows(rows_ref, e))
        total = total + dot(hidden_ref[e][:, main:], last_ref[step, e * sources : (e + 1) * sources, :])
        out_ref[:, e] = total.astype(BF).reshape(groups, units, width)


def partial_down(arrived, hidden, groups):
    sources, rows, _ = arrived.shape
    _, units, slots = hidden.shape
    width = rows // 34 * LANE
    return pl.pallas_call(
        down_kernel,
        grid=(FOLD,),
        in_specs=[
            pl.BlockSpec((sources, 128, LANE), lambda i: (0, i, 0)),
            pl.BlockSpec((sources, 64, LANE), lambda i: (0, 16, 0)),
            pl.BlockSpec(hidden.shape, lambda i: (0, 0, 0)),
        ],
        out_specs=pl.BlockSpec((groups, 2, units // groups, 512), lambda i: (0, 0, 0, i)),
        out_shape=jax.ShapeDtypeStruct((groups, 2, units // groups, width), BF),
        scratch_shapes=[pltpu.VMEM((FOLD, 2 * sources, 512), BF)],
        compiler_params=PARAMS,
        cost_estimate=pl.CostEstimate(flops=4 * slots * units * width, bytes_accessed=24 << 20, transcendentals=0),
        name="partial_down",
    )(arrived, arrived, hidden)


def gate_kernel(rows_ref, tail_ref, weight_ref, gate_ref, up_ref, grad_gate_ref, grad_up_ref, last_ref, total_ref):
    step = pl.program_id(0)
    sources = rows_ref.shape[0]
    main = sources * MAIN
    slots = gate_ref.shape[1]

    @pl.when(step == 0)
    def _():
        unfold(tail_ref, last_ref)
        total_ref[...] = jnp.zeros_like(total_ref)

    groups, _, units, width = weight_ref.shape
    for e in range(2):
        weight = weight_ref[:, e].reshape(groups * units, width)
        total_ref[e, :main] += dot(expert_rows(rows_ref, e), weight, ((1,), (1,)))
        total_ref[e, main:] += dot(last_ref[step, e * sources : (e + 1) * sources, :], weight, ((1,), (1,)))

    @pl.when(step == pl.num_programs(0) - 1)
    def _():
        place = natural(iota((slots, slots), 0), sources) == iota((slots, slots), 1)
        place = jnp.where(place, 1.0, 0.0).astype(BF)
        back = natural(iota((slots, slots), 1), sources) == iota((slots, slots), 0)
        back = jnp.where(back, 1.0, 0.0).astype(BF)
        for e in range(2):
            gate = dot(place, gate_ref[e])
            up = dot(place, up_ref[e])
            logistic = jax.nn.sigmoid(gate)
            grad = total_ref[e]
            grad_gate = (grad * up * logistic * (1.0 + gate * (1.0 - logistic))).astype(BF)
            grad_up = (grad * (gate * logistic)).astype(BF)
            grad_gate_ref[e] = dot(back, grad_gate).astype(BF)
            grad_up_ref[e] = dot(back, grad_up).astype(BF)


def gate_grads(arrived, weights, gate, up):
    sources, rows, _ = arrived.shape
    groups, _, units, width = weights.shape
    _, slots, all_units = gate.shape
    whole = pl.BlockSpec(gate.shape, lambda i: (0, 0, 0))
    return pl.pallas_call(
        gate_kernel,
        grid=(FOLD,),
        in_specs=[
            pl.BlockSpec((sources, 128, LANE), lambda i: (0, i, 0)),
            pl.BlockSpec((sources, 64, LANE), lambda i: (0, 16, 0)),
            pl.BlockSpec((groups, 2, units, 512), lambda i: (0, 0, 0, i)),
            whole,
            whole,
        ],
        out_specs=[whole, whole],
        out_shape=[jax.ShapeDtypeStruct(gate.shape, BF)] * 2,
        scratch_shapes=[
            pltpu.VMEM((FOLD, 2 * sources, 512), BF),
            pltpu.VMEM((2, slots, all_units), F32),
        ],
        compiler_params=PARAMS,
        cost_estimate=pl.CostEstimate(flops=4 * slots * all_units * width, bytes_accessed=32 << 20, transcendentals=2 * slots * all_units),
        name="gate_grads",
    )(arrived, arrived, weights, gate, up)


def on_device(grad_out, expert_ids, gate_weights, saved_gate, saved_up, down_weight):
    sources = lax.axis_size("expert")
    groups = lax.axis_size("dp")
    units, local, width = down_weight.shape
    weights = lax.all_gather(jnp.transpose(down_weight, (1, 0, 2)), "dp", axis=0, tiled=False)
    rows = dispatch(expert_ids, gate_weights, grad_out, sources)
    arrived = lax.all_to_all(rows, "expert", split_axis=0, concat_axis=0, tiled=True)
    hidden = arranged_hidden(saved_gate, saved_up, sources)
    partial = partial_down(arrived, hidden, groups)
    summed = lax.psum_scatter(
        partial.reshape(groups, local * units, width), "dp", scatter_dimension=0, tiled=True
    )
    grad_gate, grad_up = gate_grads(arrived, weights, saved_gate, saved_up)
    grad_down = jnp.transpose(summed.reshape(local, units, width), (1, 0, 2)).astype(F32)
    return (grad_gate, grad_up, grad_down)


def solution(mesh):
    in_specs = (
        P(("dp", "expert"), None),
        P(("dp", "expert"), None),
        P(("dp", "expert"), None),
        P("expert", "dp", None),
        P("expert", "dp", None),
        P("dp", "expert", None),
    )
    out_specs = (P("expert", "dp", None), P("expert", "dp", None), P("dp", "expert", None))
    return jax.shard_map(
        on_device, mesh=mesh, in_specs=in_specs, out_specs=out_specs, check_vma=False
    )
```

time: 835 us -> 336 us (0.40)
  waiting for transfers between devices: 592 us -> 244 us
  local copies, waits for them, and re-layouts: 108 us -> 8.99 us
  Pallas kernels: 0 us -> 58.5 us
  matrix products: 57 us -> 0 us
  other arithmetic: 40.5 us -> 1.75 us
  starting transfers between devices: 16.2 us -> 7.85 us
    unnamed x3 -> x2, waiting for transfers between devices: 265 us -> 0.03 us
    all_gather x1, waiting for transfers between devices: 130 us -> 0.02 us  [on_device(): lax.all_gather(jnp.transpose(down_weight, (1, 0, 2)), 'dp', axis=0, tiled...]
    reduce_scatter x0 -> x1, waiting for transfers between devices: none -> 112 us  [on_device(): lax.psum_scatter(partial.reshape(groups, local * units, width), 'dp', sca...]
    convert_element_type x5 -> x0, local copies, waits for them, and re-layouts: 66.3 us -> none  [the longest x2 34.5 us: on_device(): arrived_rows.astype(jnp.float32)]
    all_to_all x2 -> x1, waiting for transfers between devices: 197 us -> 131 us  [on_device(): lax.all_to_all(rows, 'expert', split_axis=0, concat_axis=0, tiled=True)]
    pallas_call x0 -> x4, Pallas kernels: none -> 58.5 us  [the longest x1 24.4 us: gate_grads(): pl.pallas_call(gate_kernel, grid=(FOLD,), in_specs=[pl.BlockSpec((sources...]
    dot_general x2 -> x0, matrix products: 57 us -> none  [the longest x1 28.8 us: on_device(): jnp.einsum('esf,esd->fed', hidden, dispatched, preferred_element_type=jnp...]
    unnamed x15 -> x8, local copies, waits for them, and re-layouts: 29.3 us -> 8.99 us
  transfers between devices with their start and end apart: 4 -> 3, of which waited for: 3 -> 2; matrix products, arithmetic and copies ran while one was open for 4% -> 0% of each run, Pallas kernels for 0% -> 17%
where the time goes in v1:
time: 336 us; the launch traced here: 335 us
  waiting for transfers between devices  244 us (73%)
  Pallas kernels  58.5 us (17%)
  between operations  14.1 us (4%)
  local copies, waits for them, and re-layouts  8.99 us (3%)
  starting transfers between devices  7.85 us (2%)
    all_to_all x1, waiting for transfers between devices, on_device(): lax.all_to_all(rows, 'expert', split_axis=0, concat_axis=0, tiled=True)  131 us
    reduce_scatter x1, waiting for transfers between devices, on_device(): lax.psum_scatter(partial.reshape(groups, local * units, width), 'dp', sca...  112 us
    pallas_call x1, Pallas kernels, gate_grads(): pl.pallas_call(gate_kernel, grid=(FOLD,), in_specs=[pl.BlockSpec((sources...  24.4 us
    pallas_call x1, Pallas kernels, partial_down(): pl.pallas_call(down_kernel, grid=(FOLD,), in_specs=[pl.BlockSpec((sources...  16.7 us
    pallas_call x1, Pallas kernels, dispatch(): pl.pallas_call(dispatch_kernel, grid=(steps,), in_specs=[pl.BlockSpec(ids...  12.7 us
    unnamed x8, local copies, waits for them, and re-layouts  8.99 us
    all_to_all x1, starting transfers between devices, on_device(): lax.all_to_all(rows, 'expert', split_axis=0, concat_axis=0, tiled=True)  7.59 us
  transfers between devices with their start and end apart: 3, of which 2 were waited for; matrix products, arithmetic and copies ran while one was open for 0% of the time, Pallas kernels for 17%

profile of v1, /device:TPU:8, one launch (start us, length us, event | category | flops | bytes accessed | tf_op | source)
XLA Modules:
  0.0 334.7 jit_solution(14306258240670113115)
XLA Ops:
  7.2 0.0 copy-start
  7.2 0.0 copy-start.1
  7.2 0.0 all-gather.3.cloned.1.call-start
  7.2 3.4 %copy.21 = bf16[96,2,4096]{2,0,1:T(8,128)(2,1)} copy(bf16[96,2,4096]{2,1,0:T(2,128)(2,1)} %param.11) | data formatting | bytes 3145728 | tf_op args[5]
  10.7 0.0 all-gather.3.cloned.1.call-update
  10.7 0.0 copy-done
  10.7 0.7 copy.16.ids_ref
  11.4 0.0 copy-done.1
  11.4 0.7 copy.17.gates_ref
  12.2 12.7 %dispatch.1 = bf16[32,1088,128]{2,1,0:T(8,128)(2,1)} custom-call(s32[128,8]{1,0:T(8,128)} %copy.16.ids_ref, bf16[128,8]{1,0:T(8,128)(2,1)} %copy.17.gates_ref, bf16[128,4096]{1,0:T(8,128)(2,1)} %grad_ref.1), custom_call_target="tpu_custom_call" | custom-call | flops 1140850688 | bytes 10485760 | tf_op jit(solution)/shard_map/dispatch/pallas_call | solution.py:75
  24.8 7.6 %all-to-all-start = ((bf16[32,1088,128]{2,1,0:T(8,128)(2,1)}), bf16[32,1088,128]{2,1,0:T(8,128)(2,1)}, u32[]{:S(2)}, u32[]{:S(2)}) async-start(bf16[32,1088,128]{2,1,0:T(8,128)(2,1)} %dispatch.1), calls=%async_computation | async-start | bytes 17825792 | tf_op jit(solution)/shard_map/all_to_all | solution.py:250
  32.4 0.2 reduce-scatter.2.cloned.1.call-start
  32.6 4.7 %hidden.1.hidden_ref = bf16[2,768,544]{2,1,0:T(8,128)(2,1)} custom-call(bf16[2,544,768]{2,1,0:T(8,128)(2,1)} %gate_ref.3, bf16[2,544,768]{2,1,0:T(8,128)(2,1)} %up_ref.3), custom_call_target="tpu_custom_call" | custom-call | flops 909115392 | bytes 6291456 | tf_op jit(solution)/shard_map/hidden/pallas_call | solution.py:112
  37.4 131.1 %all-to-all-done.rows_ref.tail_ref = bf16[32,1088,128]{2,1,0:T(8,128)(2,1)} async-done(((bf16[32,1088,128]{2,1,0:T(8,128)(2,1)}), bf16[32,1088,128]{2,1,0:T(8,128)(2,1)}, u32[]{:S(2)}, u32[]{:S(2)}) %all-to-all-start) | async-done | bytes 8912928 | tf_op jit(solution)/shard_map/all_to_all | solution.py:250
  168.5 16.7 %partial_down.1 = bf16[8,2,96,4096]{3,2,1,0:T(8,128)(2,1)} custom-call(bf16[32,1088,128]{2,1,0:T(8,128)(2,1)} %all-to-all-done.rows_ref.tail_ref, bf16[32,1088,128]{2,1,0:T(8,128)(2,1)} %all-to-all-done.rows_ref.tail_ref, bf16[2,768,544]{2,1,0:T(8,128)(2,1)} %hidden.1.hidden_ref), custom_call_target="tpu_custom_call" | custom-call | flops 6845104128 | bytes 25165824 | tf_op jit(solution)/shard_map/partial_down/pallas_call | solution.py:166
  185.2 0.0 reduce-scatter.2.cloned.1.call-update
  185.2 0.0 all-gather.3.cloned.1.call-done
  185.2 24.4 %gate_grads.1 = (bf16[2,544,768]{2,1,0:T(8,128)(2,1)}, bf16[2,544,768]{2,1,0:T(8,128)(2,1)}) custom-call(bf16[32,1088,128]{2,1,0:T(8,128)(2,1)} %all-to-all-done.rows_ref.tail_ref, bf16[32,1088,128]{2,1,0:T(8,128)(2,1)} %all-to-all-done.rows_ref.tail_ref, bf16[8,2,96,4096]{3,2,1,0:T(8,128)(2,1)} %bitcast.10, bf16[2,544,768]{2,1,0:T(8,128)(2,1)} %gate_ref.3, ...), custom_call_target="tpu_custom_call" | custom-call | flops 6845104128 | bytes 33554432 | tf_op jit(solution)/shard_map/gate_grads/pallas_call | solution.py:222
  209.6 112.4 %reduce-scatter.2.cloned.1.call-done = bf16[1,192,4096]{2,1,0:T(8,128)(2,1)} async-done(((bf16[8,192,4096]{2,1,0:T(8,128)(2,1)}), bf16[1,192,4096]{2,1,0:T(8,128)(2,1)}) %reduce-scatter.2.cloned.1.call-update) | async-done | bytes 1572880 | tf_op jit(solution)/shard_map/reduce_scatter | solution.py:253
  322.0 1.7 convert_bitcast_fusion
  323.8 4.1 %copy.19 = f32[96,2,4096]{2,1,0:T(2,128)} copy(f32[96,2,4096]{2,0,1:T(8,128)S(1)} %convert_bitcast_fusion) | data formatting | bytes 6291456
Async XLA Ops:
  7.2 3.5 %copy-start = (s32[128,8]{0,1:T(8,128)S(1)}, s32[128,8]{0,1:T(8,128)}, u32[]{:S(2)}) copy-start(s32[128,8]{0,1:T(8,128)} %param.7) | copy-start | bytes 12292
  7.2 4.3 %copy-start.1 = (bf16[128,8]{0,1:T(8,128)(2,1)S(1)}, bf16[128,8]{0,1:T(8,128)(2,1)}, u32[]{:S(2)}) copy-start(bf16[128,8]{0,1:T(8,128)(2,1)} %param.8) | copy-start | bytes 6148
  7.2 178.0 %all-gather.3.cloned.1.call-start = ((), (), s32[]{:S(2)}) async-start(), calls=%async_computation.3 | async-start | bytes 14155776 | tf_op jit(solution)/shard_map/all_gather | solution.py:248
  24.8 143.6 %all-to-all-start = ((bf16[32,1088,128]{2,1,0:T(8,128)(2,1)}), bf16[32,1088,128]{2,1,0:T(8,128)(2,1)}, u32[]{:S(2)}, u32[]{:S(2)}) async-start(bf16[32,1088,128]{2,1,0:T(8,128)(2,1)} %dispatch.1), calls=%async_computation | async-start | bytes 17825792 | tf_op jit(solution)/shard_map/all_to_all | solution.py:250
  32.4 289.6 %reduce-scatter.2.cloned.1.call-start = ((), (), s32[]{:S(2)}) async-start(), calls=%async_computation.2 | async-start | bytes 14155776 | tf_op jit(solution)/shard_map/reduce_scatter | solution.py:253
Sparse Core Ops, SparseCore 0:
  10.8 136.3 all-gather.2
  185.3 136.6 reduce-scatter.1

commit v2 on v0

v2 whole, which is shorter than its diff:
```python
import functools

import jax
import jax.numpy as jnp
from jax import lax
from jax.experimental import pallas as pl
from jax.experimental.pallas import tpu as pltpu
from jax.sharding import PartitionSpec as P

BF = jnp.bfloat16
F32 = jnp.float32
LANE = 128
MAIN = 16
FOLD = 8
WIDE = FOLD * LANE
BLOCK = 2 * MAIN * FOLD + 2 * FOLD
PARAMS = pltpu.CompilerParams(vmem_limit_bytes=56 * 1024 * 1024)


def dot(a, b, dims=((1,), (0,))):
    return lax.dot_general(a, b, (dims, ((), ())), preferred_element_type=F32)


def iota(shape, dim):
    return lax.broadcasted_iota(jnp.int32, shape, dim)


def dispatch_kernel(ids_ref, gates_ref, grad_ref, out_ref, main_ref, tail_ref):
    top, tokens = ids_ref.shape
    dests = out_ref.shape[0]
    experts = 2 * dests

    @pl.when(pl.program_id(0) == 0)
    def _():
        expert = iota((experts, tokens), 0)
        member = jnp.zeros((experts, tokens), F32)
        gate = jnp.zeros((experts, tokens), F32)
        gates = gates_ref[...].astype(F32)
        for k in range(top):
            hit = ids_ref[k : k + 1, :] == expert
            member = jnp.where(hit, 1.0, member)
            gate = jnp.where(hit, gates[k : k + 1, :], gate)
        earlier = jnp.where(iota((tokens, tokens), 0) < iota((tokens, tokens), 1), 1.0, 0.0)
        rank = dot(member.astype(BF), earlier.astype(BF))
        rank = jnp.where(member > 0.0, rank, -1.0)
        slots = iota((experts, MAIN, tokens), 1).astype(F32)
        chosen = jnp.where(rank[:, None, :] == slots, gate[:, None, :], 0.0)
        main_ref[...] = chosen.reshape(experts * MAIN, tokens).astype(BF)
        last = jnp.where(rank == float(MAIN), gate, 0.0)
        last = jnp.broadcast_to(last[:, None, :], (experts, FOLD, tokens)).reshape(experts * FOLD, tokens)
        rows = iota((experts * FOLD, tokens), 0) % FOLD
        for k in range(FOLD):
            tail_ref[:, k * tokens : (k + 1) * tokens] = jnp.where(rows == k, last, 0.0).astype(BF)

    for pair in range(FOLD // 2):
        rows = dot(main_ref[...], grad_ref[:, pair * 256 : (pair + 1) * 256]).astype(BF)
        for k in range(2):
            at = (2 * pair + k) * 2 * MAIN
            out_ref[:, at : at + 2 * MAIN, :] = rows[:, k * LANE : (k + 1) * LANE].reshape(dests, 2 * MAIN, LANE)
    stacked = jnp.concatenate([grad_ref[:, k * LANE : (k + 1) * LANE] for k in range(FOLD)], axis=0)
    rows = dot(tail_ref[...], stacked).astype(BF)
    out_ref[:, 2 * MAIN * FOLD :, :] = rows.reshape(dests, 2 * FOLD, LANE)


def dispatch(ids, gates, grad, dests, first, count):
    tokens, _ = grad.shape
    ids, gates = jnp.transpose(ids), jnp.transpose(gates)
    return pl.pallas_call(
        dispatch_kernel,
        grid=(count,),
        in_specs=[
            pl.BlockSpec(ids.shape, lambda i: (0, 0)),
            pl.BlockSpec(gates.shape, lambda i: (0, 0)),
            pl.BlockSpec((tokens, WIDE), lambda i: (0, first + i)),
        ],
        out_specs=pl.BlockSpec((dests, BLOCK, LANE), lambda i: (0, i, 0)),
        out_shape=jax.ShapeDtypeStruct((dests, count * BLOCK, LANE), BF),
        scratch_shapes=[
            pltpu.VMEM((2 * dests * MAIN, tokens), BF),
            pltpu.VMEM((2 * dests * FOLD, FOLD * tokens), BF),
        ],
        compiler_params=PARAMS,
        cost_estimate=pl.CostEstimate(
            flops=count * 2 * 1088 * 128 * WIDE, bytes_accessed=count * 3 << 20, transcendentals=0
        ),
        name="dispatch",
    )(ids, gates, grad)


def natural(order, sources):
    main = sources * MAIN
    return jnp.where(order < main, (order // MAIN) * (MAIN + 1) + order % MAIN, (order - main) * (MAIN + 1) + MAIN)


def arrange_kernel(sources, gate_ref, up_ref, hidden_ref, gate_out_ref, up_out_ref):
    gate = gate_ref[0].astype(F32)
    slots = gate.shape[0]
    hidden = (gate * jax.nn.sigmoid(gate) * up_ref[0].astype(F32)).astype(BF)
    place = natural(iota((slots, slots), 1), sources) == iota((slots, slots), 0)
    place = jnp.where(place, 1.0, 0.0).astype(BF)
    hidden_ref[0] = dot(hidden, place, ((0,), (0,))).astype(BF)
    place = natural(iota((slots, slots), 0), sources) == iota((slots, slots), 1)
    place = jnp.where(place, 1.0, 0.0).astype(BF)
    gate_out_ref[0] = dot(place, gate_ref[0]).astype(BF)
    up_out_ref[0] = dot(place, up_ref[0]).astype(BF)


def arrange(gate, up, sources):
    local, slots, units = gate.shape
    spec = pl.BlockSpec((1, slots, units), lambda e: (e, 0, 0))
    return pl.pallas_call(
        functools.partial(arrange_kernel, sources),
        grid=(local,),
        in_specs=[spec, spec],
        out_specs=[pl.BlockSpec((1, units, slots), lambda e: (e, 0, 0)), spec, spec],
        out_shape=[jax.ShapeDtypeStruct((local, units, slots), BF)] + [jax.ShapeDtypeStruct(gate.shape, BF)] * 2,
        compiler_params=PARAMS,
        cost_estimate=pl.CostEstimate(flops=12 * slots * slots * units, bytes_accessed=9 << 20, transcendentals=0),
        name="arrange",
    )(gate, up)


def expert_rows(rows_ref, expert, out_ref):
    sources = rows_ref.shape[0]
    main = sources * MAIN
    for k in range(FOLD):
        at = (2 * k + expert) * MAIN
        out_ref[:main, k * LANE : (k + 1) * LANE] = rows_ref[:, at : at + MAIN, :].reshape(main, LANE)
    at = 2 * MAIN * FOLD
    folded = rows_ref[:, at : at + 2 * FOLD, :].reshape(sources * 2 * FOLD, LANE)
    row = iota((FOLD * sources, sources * 2 * FOLD), 0)
    column = iota((FOLD * sources, sources * 2 * FOLD), 1)
    pick = column == (row % sources) * 2 * FOLD + expert * FOLD + row // sources
    last = dot(jnp.where(pick, 1.0, 0.0).astype(BF), folded).astype(BF)
    for k in range(FOLD):
        out_ref[main:, k * LANE : (k + 1) * LANE] = last[k * sources : (k + 1) * sources]


def down_kernel(place_ref, rows_ref, hidden_ref, slots_ref, rest_ref, first_ref):
    e = pl.program_id(1)
    groups = rest_ref.shape[0]
    units = hidden_ref.shape[1] // groups
    for local in range(2):

        @pl.when(e == local)
        def _():
            expert_rows(rows_ref, local, slots_ref.at[0])

    for n in range(WIDE // 256):
        columns = slice(n * 256, (n + 1) * 256)
        total = dot(hidden_ref[0], slots_ref[0, :, columns]).astype(BF)
        for c in range(groups):
            turn = lax.rem(place_ref[1] * (place_ref[0] - c) - 1 + 2 * groups, groups)
            rest_ref[turn, :, columns] = total[c * units : (c + 1) * units]
    first_ref[...] = rest_ref[0]


def partial_down(place, arrived, hidden, groups, at, count):
    sources, _, _ = arrived.shape
    _, units, slots = hidden.shape
    rows = units // groups
    return pl.pallas_call(
        down_kernel,
        grid=(count, 2),
        in_specs=[
            pl.BlockSpec(memory_space=pltpu.SMEM),
            pl.BlockSpec((sources, BLOCK, LANE), lambda q, e: (0, at + q, 0)),
            pl.BlockSpec((1, units, slots), lambda q, e: (e, 0, 0)),
        ],
        out_specs=[
            pl.BlockSpec((1, slots, WIDE), lambda q, e: (e, 0, q)),
            pl.BlockSpec((groups, rows, WIDE), lambda q, e: (0, e, q)),
            pl.BlockSpec((rows, WIDE), lambda q, e: (e, q)),
        ],
        out_shape=[
            jax.ShapeDtypeStruct((2, slots, count * WIDE), BF),
            jax.ShapeDtypeStruct((groups, 2 * rows, count * WIDE), BF),
            jax.ShapeDtypeStruct((2 * rows, count * WIDE), BF),
        ],
        compiler_params=PARAMS,
        cost_estimate=pl.CostEstimate(
            flops=count * 4 * slots * units * WIDE, bytes_accessed=count * 9 << 20, transcendentals=0
        ),
        name="partial_down",
    )(place, arrived, hidden)


def hidden_grad_kernel(count, *refs):
    weight_ref, total_ref = refs[-2:]
    step = pl.program_id(0)
    groups, _, units, width = weight_ref.shape
    steps = 2 * WIDE // width
    slots_refs = refs[1 : 1 + count]

    @pl.when(step == 0)
    def _():
        total_ref[...] = refs[-3][...] if len(refs) == count + 4 else jnp.zeros_like(total_ref)

    for k, slots_ref in enumerate(slots_refs):

        @pl.when(step // (steps // count) == k)
        def _():
            weight = weight_ref[:, 0].reshape(groups * units, width)
            for n in range(0, groups * units, 256):
                total_ref[:, n : n + 256] += dot(slots_ref[0], weight[n : n + 256], ((1,), (1,)))


def hidden_grad(after, rows, weights, half, expert, before=()):
    groups, _, units, _ = weights.shape
    slots = rows[0].shape[1]
    width = WIDE // 2
    count = len(rows)
    each = 2 * WIDE // width // count
    whole = pl.BlockSpec((slots, groups * units), lambda k: (0, 0))
    specs = [
        pl.BlockSpec((1, slots, width), lambda k, j=j: (expert, 0, jnp.clip(k - j * each, 0, each - 1)))
        for j in range(count)
    ]
    return pl.pallas_call(
        functools.partial(hidden_grad_kernel, count),
        grid=(each * count,),
        in_specs=[pl.BlockSpec(memory_space=pltpu.SMEM)]
        + specs
        + [whole] * len(before)
        + [pl.BlockSpec((groups, 1, units, width), lambda k: (0, expert, 0, half * each * count + k))],
        out_specs=whole,
        out_shape=jax.ShapeDtypeStruct((slots, groups * units), F32),
        compiler_params=PARAMS,
        cost_estimate=pl.CostEstimate(
            flops=4 * slots * groups * units * WIDE, bytes_accessed=9 << 20, transcendentals=0
        ),
        name="hidden_grad",
    )(after, *rows, *before, weights)


def gate_grads_kernel(sources, after_ref, total_ref, gate_ref, up_ref, *refs):
    grad_gate_ref, grad_up_ref = refs[-2:]
    slots, _ = total_ref.shape
    back = natural(iota((slots, slots), 1), sources) == iota((slots, slots), 0)
    back = jnp.where(back, 1.0, 0.0).astype(BF)
    gate = gate_ref[0].astype(F32)
    up = up_ref[0].astype(F32)
    logistic = jax.nn.sigmoid(gate)
    grad = total_ref[...]
    grad_gate = (grad * up * logistic * (1.0 + gate * (1.0 - logistic))).astype(BF)
    grad_up = (grad * (gate * logistic)).astype(BF)
    grad_gate_ref[0] = dot(back, grad_gate).astype(BF)
    grad_up_ref[0] = dot(back, grad_up).astype(BF)


def gate_grads(after, total, gate, up, sources, expert, done=()):
    one = pl.BlockSpec((1,) + gate.shape[1:], lambda i: (expert, 0, 0))
    return pl.pallas_call(
        functools.partial(gate_grads_kernel, sources),
        grid=(1,),
        in_specs=[
            pl.BlockSpec(memory_space=pltpu.SMEM),
            pl.BlockSpec(total.shape, lambda i: (0, 0)),
            one,
            one,
        ]
        + [pl.BlockSpec(memory_space=pl.ANY)] * len(done),
        out_specs=[one, one],
        out_shape=[jax.ShapeDtypeStruct(gate.shape, BF)] * 2,
        input_output_aliases={4 + k: k for k in range(len(done))},
        compiler_params=PARAMS,
        cost_estimate=pl.CostEstimate(flops=4 * 544 * 544 * 768, bytes_accessed=5 << 20, transcendentals=0),
        name="gate_grads",
    )(after, total, gate, up, *done)


def final_kernel(after_ref, own_ref, arrived_ref, *refs):
    out_ref = refs[-1]
    units, _, _ = out_ref.shape
    value = arrived_ref[...].astype(F32) + own_ref[0].astype(F32)
    for e in range(2):
        out_ref[:, e, :] = value[e * units : (e + 1) * units]


def final(after, arrived, rest, shape, at, done=()):
    groups, rows, width = rest.shape
    return pl.pallas_call(
        final_kernel,
        grid=(width // WIDE,),
        in_specs=[
            pl.BlockSpec(memory_space=pltpu.SMEM),
            pl.BlockSpec((1, rows, WIDE), lambda i: (groups - 1, 0, i)),
            pl.BlockSpec((rows, WIDE), lambda i: (0, i)),
        ]
        + [pl.BlockSpec(memory_space=pl.ANY)] * len(done),
        out_specs=pl.BlockSpec((shape[0], 2, WIDE), lambda i: (0, 0, at + i)),
        out_shape=jax.ShapeDtypeStruct(shape, F32),
        input_output_aliases={3 + k: k for k in range(len(done))},
        compiler_params=PARAMS,
        cost_estimate=pl.CostEstimate(flops=rows * width, bytes_accessed=3 << 20, transcendentals=0),
        name="final",
    )(after, rest, arrived, *done)


class Clock:
    def __init__(self, value):
        self.value = value

    def __call__(self, value):
        value, self.value = lax.optimization_barrier((value, self.value))
        return value


class Ring:
    def __init__(self, clock, rest, blocks):
        self.clock, self.rest, self.turn = clock, rest, 0
        groups, members = lax.axis_size("dp"), lax.axis_size("expert")
        self.pairs = [
            (g * members + j, (g + 1 - 2 * (j % 2)) % groups * members + j)
            for g in range(groups)
            for j in range(members)
        ]
        self.send(blocks)

    def send(self, blocks):
        self.got = lax.ppermute(blocks, ("dp", "expert"), self.pairs)

    def step(self):
        self.turn += 1
        self.send(self.clock(self.clock(self.got) + self.rest[self.turn]))


def on_device(grad_out, expert_ids, gate_weights, saved_gate, saved_up, down_weight):
    sources = lax.axis_size("expert")
    groups = lax.axis_size("dp")
    units, local, width = down_weight.shape
    place = jnp.stack([lax.axis_index("dp"), 1 - 2 * (lax.axis_index("expert") % 2)]).astype(jnp.int32)
    clock = Clock(place)

    def exchange(rows):
        return lax.all_to_all(rows, "expert", split_axis=0, concat_axis=0, tiled=True)

    weights = lax.all_gather(jnp.transpose(down_weight, (1, 0, 2)), "dp", axis=0, tiled=False)
    arrived = [exchange(dispatch(expert_ids, gate_weights, grad_out, sources, at, 2)) for at in (0, 2)]
    hidden, gate, up = arrange(saved_gate, saved_up, sources)

    slots, rings, total = [], [], [(), ()]
    for half in range(2):
        rows, rest, sent = partial_down(place, clock(arrived[half]), hidden, groups, 0, 2)
        slots.append(rows)
        rings.append(Ring(clock, rest, clock(sent)))

    def hidden_piece(half, e):
        piece = hidden_grad(clock.value, [slots[half]], weights, half, e, total[e])
        total[e] = (clock(piece),)

    def gate_piece(e, done):
        return clock(gate_grads(clock.value, total[e][0], gate, up, sources, e, done))

    grads = ()
    for turn in range(1, groups - 1):
        rings[0].step()
        if turn in (1, 2, 4, 5):
            hidden_piece((turn - 1) % 3, turn // 3)
        else:
            grads = gate_piece(turn // 3 - 1, grads)
        rings[1].step()
    out_shape, grad_down = (units, local, width), ()
    for half in range(2):
        got = clock(rings[half].got)
        grad_down = (final(clock.value, got, rings[half].rest, out_shape, 2 * half, grad_down),)
    return (grads[0], grads[1], grad_down[0])


def solution(mesh):
    in_specs = (
        P(("dp", "expert"), None),
        P(("dp", "expert"), None),
        P(("dp", "expert"), None),
        P("expert", "dp", None),
        P("expert", "dp", None),
        P("dp", "expert", None),
    )
    out_specs = (P("expert", "dp", None), P("expert", "dp", None), P("dp", "expert", None))
    return jax.shard_map(
        on_device, mesh=mesh, in_specs=in_specs, out_specs=out_specs, check_vma=False
    )
```

time: 835 us -> 288 us (0.34)
  waiting for transfers between devices: 592 us -> 142 us
  local copies, waits for them, and re-layouts: 108 us -> 6.14 us
  Pallas kernels: 0 us -> 81.8 us
  matrix products: 57 us -> 0 us
  other arithmetic: 40.5 us -> 23 us
    unnamed x3 -> x1, waiting for transfers between devices: 265 us -> 0.02 us
    all_gather x1, waiting for transfers between devices: 130 us -> 0.01 us  [on_device(): lax.all_gather(jnp.transpose(down_weight, (1, 0, 2)), 'dp', axis=0, tiled...]
    all_to_all x2, waiting for transfers between devices: 197 us -> 88.4 us  [exchange(): lax.all_to_all(rows, 'expert', split_axis=0, concat_axis=0, tiled=True)]
    pallas_call x0 -> x13, Pallas kernels: none -> 81.8 us  [the longest x4 25.4 us: hidden_grad(): pl.pallas_call(functools.partial(hidden_grad_kernel, count), grid=(each *...]
    convert_element_type x5 -> x0, local copies, waits for them, and re-layouts: 66.3 us -> none  [the longest x2 34.5 us: on_device(): arrived_rows.astype(jnp.float32)]
    dot_general x2 -> x0, matrix products: 57 us -> none  [the longest x1 28.8 us: on_device(): jnp.einsum('esf,esd->fed', hidden, dispatched, preferred_element_type=jnp...]
    ppermute x0 -> x14, waiting for transfers between devices: none -> 53.1 us  [send(): self.got = lax.ppermute(blocks, ('dp', 'expert'), self.pairs)]
    unnamed x15 -> x13, local copies, waits for them, and re-layouts: 29.3 us -> 6.14 us
  transfers between devices with their start and end apart: 4 -> 17, of which waited for: 3 -> 13; matrix products, arithmetic and copies ran while one was open for 4% -> 8% of each run, Pallas kernels for 0% -> 28%
where the time goes in v2:
time: 288 us; the launch traced here: 287 us
  waiting for transfers between devices  142 us (49%)
  Pallas kernels  81.8 us (28%)
  other arithmetic  23 us (8%)
  starting transfers between devices  20.2 us (7%)
  between operations  14.1 us (5%)
  local copies, waits for them, and re-layouts  6.14 us (2%)
    all_to_all x2, waiting for transfers between devices, exchange(): lax.all_to_all(rows, 'expert', split_axis=0, concat_axis=0, tiled=True)  88.4 us
    ppermute x14, waiting for transfers between devices, send(): self.got = lax.ppermute(blocks, ('dp', 'expert'), self.pairs)  53.1 us
    pallas_call x4, Pallas kernels, hidden_grad(): pl.pallas_call(functools.partial(hidden_grad_kernel, count), grid=(each *...  25.4 us
    pallas_call x2, Pallas kernels, partial_down(): pl.pallas_call(down_kernel, grid=(count, 2), in_specs=[pl.BlockSpec(memor...  24.5 us
    add x12, other arithmetic, step(): self.send(self.clock(self.clock(self.got) + self.rest[self.turn]))  22.4 us
    all_to_all x2, starting transfers between devices, exchange(): lax.all_to_all(rows, 'expert', split_axis=0, concat_axis=0, tiled=True)  12.2 us
    pallas_call x2, Pallas kernels, dispatch(): pl.pallas_call(dispatch_kernel, grid=(count,), in_specs=[pl.BlockSpec(ids...  10.2 us
    pallas_call x2, Pallas kernels, gate_grads(): pl.pallas_call(functools.partial(gate_grads_kernel, sources), grid=(1,),...  9.25 us
  transfers between devices with their start and end apart: 17, of which 13 were waited for; matrix products, arithmetic and copies ran while one was open for 8% of the time, Pallas kernels for 28%

profile of v2, /device:TPU:8, one launch (start us, length us, event | category | flops | bytes accessed | tf_op | source)
XLA Modules:
  0.0 286.7 jit_solution(7257103077745856316)
XLA Ops:
  7.2 3.4 %copy.15 = bf16[96,2,4096]{2,0,1:T(8,128)(2,1)} copy(bf16[96,2,4096]{2,1,0:T(2,128)(2,1)} %param.11) | data formatting | bytes 3145728 | tf_op args[5]
  10.7 5.1 %dispatch.2 = bf16[32,544,128]{2,1,0:T(8,128)(2,1)} custom-call(s32[8,128]{1,0:T(8,128)} %bitcast.39, bf16[8,128]{1,0:T(8,128)(2,1)} %bitcast.41, bf16[128,4096]{1,0:T(8,128)(2,1)} %grad_ref.3), custom_call_target="tpu_custom_call" | custom-call | flops 570425344 | bytes 6291456 | tf_op jit(solution)/shard_map/dispatch/pallas_call | solution.py:68
  15.8 7.6 %all-to-all-start = ((bf16[32,544,128]{2,1,0:T(8,128)(2,1)}), bf16[32,544,128]{2,1,0:T(8,128)(2,1)}, u32[]{:S(2)}, u32[]{:S(2)}) async-start(bf16[32,544,128]{2,1,0:T(8,128)(2,1)} %dispatch.2), calls=%async_computation | async-start | bytes 8912896 | tf_op jit(solution)/shard_map/all_to_all | solution.py:336
  23.4 5.0 %dispatch.3 = bf16[32,544,128]{2,1,0:T(8,128)(2,1)} custom-call(s32[8,128]{1,0:T(8,128)} %bitcast.40, bf16[8,128]{1,0:T(8,128)(2,1)} %bitcast.42, bf16[128,4096]{1,0:T(8,128)(2,1)} %grad_ref.3), custom_call_target="tpu_custom_call" | custom-call | flops 570425344 | bytes 6291456 | tf_op jit(solution)/shard_map/dispatch/pallas_call | solution.py:68
  28.4 53.9 %all-to-all-done.rows_ref = bf16[32,544,128]{2,1,0:T(8,128)(2,1)} async-done(((bf16[32,544,128]{2,1,0:T(8,128)(2,1)}), bf16[32,544,128]{2,1,0:T(8,128)(2,1)}, u32[]{:S(2)}, u32[]{:S(2)}) %all-to-all-start) | async-done | bytes 4456480 | tf_op jit(solution)/shard_map/all_to_all | solution.py:336
  82.3 4.7 %all-to-all-start.1 = ((bf16[32,544,128]{2,1,0:T(8,128)(2,1)}), bf16[32,544,128]{2,1,0:T(8,128)(2,1)}, u32[]{:S(2)}, u32[]{:S(2)}) async-start(bf16[32,544,128]{2,1,0:T(8,128)(2,1)} %dispatch.3), calls=%async_computation.1 | async-start | bytes 8912896 | tf_op jit(solution)/shard_map/all_to_all | solution.py:336
  87.6 7.5 %arrange.1 = (bf16[2,768,544]{2,1,0:T(8,128)(2,1)}, bf16[2,544,768]{2,1,0:T(8,128)(2,1)}, bf16[2,544,768]{2,1,0:T(8,128)(2,1)}) custom-call(bf16[2,544,768]{2,1,0:T(8,128)(2,1)} %gate_ref.1, bf16[2,544,768]{2,1,0:T(8,128)(2,1)} %up_ref.1), custom_call_target="tpu_custom_call" | custom-call | flops 2727346176 | bytes 9437184 | tf_op jit(solution)/shard_map/arrange/pallas_call | solution.py:111
  95.1 12.3 %partial_down.2 = (bf16[2,544,2048]{2,1,0:T(8,128)(2,1)}, bf16[8,192,2048]{2,1,0:T(8,128)(2,1)}, bf16[192,2048]{1,0:T(8,128)(2,1)}) custom-call(s32[2]{0:T(128)} %pad_add_fusion.place_ref.refs_0_.after_ref, bf16[32,544,128]{2,1,0:T(8,128)(2,1)} %all-to-all-done.rows_ref, bf16[2,768,544]{2,1,0:T(8,128)(2,1)} %get-tuple-element.91.hidden_ref), custom_call_target="tpu_custom_call" | custom-call | flops 3422552064 | bytes 18874368 | tf_op jit(solution)/shard_map/partial_down/pallas_call | solution.py:162
  107.4 2.0 collective-permute-start
  109.4 34.5 %all-to-all-done.1.rows_ref = bf16[32,544,128]{2,1,0:T(8,128)(2,1)} async-done(((bf16[32,544,128]{2,1,0:T(8,128)(2,1)}), bf16[32,544,128]{2,1,0:T(8,128)(2,1)}, u32[]{:S(2)}, u32[]{:S(2)}) %all-to-all-start.1) | async-done | bytes 4456480 | tf_op jit(solution)/shard_map/all_to_all | solution.py:336
  143.9 12.2 %partial_down.3 = (bf16[2,544,2048]{2,1,0:T(8,128)(2,1)}, bf16[8,192,2048]{2,1,0:T(8,128)(2,1)}, bf16[192,2048]{1,0:T(8,128)(2,1)}) custom-call(s32[2]{0:T(128)} %pad_add_fusion.place_ref.refs_0_.after_ref, bf16[32,544,128]{2,1,0:T(8,128)(2,1)} %all-to-all-done.1.rows_ref, bf16[2,768,544]{2,1,0:T(8,128)(2,1)} %get-tuple-element.91.hidden_ref), custom_call_target="tpu_custom_call" | custom-call | flops 3422552064 | bytes 18874368 | tf_op jit(solution)/shard_map/partial_down/pallas_call | solution.py:162
  156.1 1.9 collective-permute-start.2
  158.0 0.9 copy-done.2
  158.9 2.5 bitcast_add_fusion.11
  161.4 1.9 collective-permute-start.1
  163.3 6.2 %hidden_grad.4.refs_2_ = f32[544,768]{1,0:T(8,128)} custom-call(s32[2]{0:T(128)} %pad_add_fusion.place_ref.refs_0_.after_ref, bf16[2,544,2048]{2,1,0:T(8,128)(2,1)} %get-tuple-element.106.refs_1_, bf16[8,2,96,4096]{3,2,1,0:T(8,128)(2,1)} %bitcast.32), custom_call_target="tpu_custom_call" | custom-call | flops 1711276032 | bytes 9437184 | tf_op jit(solution)/shard_map/hidden_grad/pallas_call | solution.py:219
  169.5 2.6 collective-permute-done.2
  172.1 2.1 bitcast_add_fusion.10
  174.2 6.4 %collective-permute-done.1 = bf16[192,2048]{1,0:T(8,128)(2,1)} collective-permute-done((bf16[192,2048]{1,0:T(8,128)(2,1)}, bf16[192,2048]{1,0:T(8,128)(2,1)}, u32[]{:S(2)}, u32[]{:S(2)}) %collective-permute-start.1) | collective-permute-done | bytes 786464 | tf_op jit(solution)/shard_map/ppermute | solution.py:321
  180.7 2.1 bitcast_add_fusion.9
  182.8 6.6 %hidden_grad.5.total_ref = f32[544,768]{1,0:T(8,128)} custom-call(s32[2]{0:T(128)} %pad_add_fusion.place_ref.refs_0_.after_ref, bf16[2,544,2048]{2,1,0:T(8,128)(2,1)} %get-tuple-element.117.refs_1_, f32[544,768]{1,0:T(8,128)} %hidden_grad.4.refs_2_, bf16[8,2,96,4096]{3,2,1,0:T(8,128)(2,1)} %bitcast.33), custom_call_target="tpu_custom_call" | custom-call | flops 1711276032 | bytes 9437184 | tf_op jit(solution)/shard_map/hidden_grad/pallas_call | solution.py:219
  189.4 1.5 bitcast_add_fusion.8
  190.9 6.6 %collective-permute-done.3 = bf16[192,2048]{1,0:T(8,128)(2,1)} collective-permute-done((bf16[192,2048]{1,0:T(8,128)(2,1)}, bf16[192,2048]{1,0:T(8,128)(2,1)}, u32[]{:S(2)}, u32[]{:S(2)}) %collective-permute-start.3) | collective-permute-done | bytes 786464 | tf_op jit(solution)/shard_map/ppermute | solution.py:321
  197.5 2.1 bitcast_add_fusion.7
  199.6 4.6 %gate_grads.2 = (bf16[2,544,768]{2,1,0:T(8,128)(2,1)}, bf16[2,544,768]{2,1,0:T(8,128)(2,1)}) custom-call(s32[2]{0:T(128)} %pad_add_fusion.place_ref.refs_0_.after_ref, f32[544,768]{1,0:T(8,128)} %hidden_grad.5.total_ref, bf16[2,544,768]{2,1,0:T(8,128)(2,1)} %get-tuple-element.129.gate_ref, bf16[2,544,768]{2,1,0:T(8,128)(2,1)} %get-tuple-element.130.up_ref), custom_call_target="tpu_custom_call" | custom-call | flops 909115392 | bytes 5242880 | tf_op jit(solution)/shard_map/gate_grads/pallas_call | solution.py:253
  204.2 1.7 collective-permute-done.6
  206.0 1.5 bitcast_add_fusion.6
  207.5 6.9 %collective-permute-done.5 = bf16[192,2048]{1,0:T(8,128)(2,1)} collective-permute-done((bf16[192,2048]{1,0:T(8,128)(2,1)}, bf16[192,2048]{1,0:T(8,128)(2,1)}, u32[]{:S(2)}, u32[]{:S(2)}) %collective-permute-start.5) | collective-permute-done | bytes 786464 | tf_op jit(solution)/shard_map/ppermute | solution.py:321
  214.4 2.1 bitcast_add_fusion.5
  216.5 6.0 %hidden_grad.6.refs_2_ = f32[544,768]{1,0:T(8,128)} custom-call(s32[2]{0:T(128)} %pad_add_fusion.place_ref.refs_0_.after_ref, bf16[2,544,2048]{2,1,0:T(8,128)(2,1)} %get-tuple-element.106.refs_1_, bf16[8,2,96,4096]{3,2,1,0:T(8,128)(2,1)} %bitcast.34), custom_call_target="tpu_custom_call" | custom-call | flops 1711276032 | bytes 9437184 | tf_op jit(solution)/shard_map/hidden_grad/pallas_call | solution.py:219
  222.8 1.5 bitcast_add_fusion.4
  224.3 0.6 collective-permute-start.10
  224.9 6.3 %collective-permute-done.7 = bf16[192,2048]{1,0:T(8,128)(2,1)} collective-permute-done((bf16[192,2048]{1,0:T(8,128)(2,1)}, bf16[192,2048]{1,0:T(8,128)(2,1)}, u32[]{:S(2)}, u32[]{:S(2)}) %collective-permute-start.7) | collective-permute-done | bytes 786464 | tf_op jit(solution)/shard_map/ppermute | solution.py:321
  231.2 2.1 bitcast_add_fusion.3
  233.4 6.6 %hidden_grad.7.total_ref = f32[544,768]{1,0:T(8,128)} custom-call(s32[2]{0:T(128)} %pad_add_fusion.place_ref.refs_0_.after_ref, bf16[2,544,2048]{2,1,0:T(8,128)(2,1)} %get-tuple-element.117.refs_1_, f32[544,768]{1,0:T(8,128)} %hidden_grad.6.refs_2_, bf16[8,2,96,4096]{3,2,1,0:T(8,128)(2,1)} %bitcast.35), custom_call_target="tpu_custom_call" | custom-call | flops 1711276032 | bytes 9437184 | tf_op jit(solution)/shard_map/hidden_grad/pallas_call | solution.py:219
  240.0 1.5 bitcast_add_fusion.2
  241.4 1.1 collective-permute-start.11
  242.5 5.5 %collective-permute-done.9 = bf16[192,2048]{1,0:T(8,128)(2,1)} collective-permute-done((bf16[192,2048]{1,0:T(8,128)(2,1)}, bf16[192,2048]{1,0:T(8,128)(2,1)}, u32[]{:S(2)}, u32[]{:S(2)}) %collective-permute-start.9) | collective-permute-done | bytes 786464 | tf_op jit(solution)/shard_map/ppermute | solution.py:321
  248.1 2.1 bitcast_add_fusion.1
  250.2 4.7 %gate_grads.3 = (bf16[2,544,768]{2,1,0:T(8,128)(2,1)}, bf16[2,544,768]{2,1,0:T(8,128)(2,1)}) custom-call(s32[2]{0:T(128)} %pad_add_fusion.place_ref.refs_0_.after_ref, f32[544,768]{1,0:T(8,128)} %hidden_grad.7.total_ref, bf16[2,544,768]{2,1,0:T(8,128)(2,1)} %get-tuple-element.129.gate_ref, ...), custom_call_target="tpu_custom_call", output_to_operand_aliasing={{0}: (4, {}), {1}: (5, {})} | custom-call | flops 909115392 | bytes 5242880 | tf_op jit(solution)/shard_map/gate_grads/pallas_call | solution.py:253
  254.9 1.7 collective-permute-done.11
  256.5 1.5 bitcast_add_fusion
  258.1 10.0 %collective-permute-done.13.arrived_ref = bf16[192,2048]{1,0:T(8,128)(2,1)S(1)} collective-permute-done((bf16[192,2048]{1,0:T(8,128)(2,1)S(1)}, bf16[192,2048]{1,0:T(8,128)(2,1)S(1)}, u32[]{:S(2)}, u32[]{:S(2)}) %collective-permute-start.13) | collective-permute-done | bytes 786464 | tf_op jit(solution)/shard_map/ppermute | solution.py:321
  268.1 0.9 copy-done
  269.0 2.5 final.2.refs_0_
  271.4 5.0 %collective-permute-done.12.arrived_ref = bf16[192,2048]{1,0:T(8,128)(2,1)S(1)} collective-permute-done((bf16[192,2048]{1,0:T(8,128)(2,1)S(1)}, bf16[192,2048]{1,0:T(8,128)(2,1)S(1)}, u32[]{:S(2)}, u32[]{:S(2)}) %collective-permute-start.12) | collective-permute-done | bytes 786464 | tf_op jit(solution)/shard_map/ppermute | solution.py:321
  276.5 0.9 copy-done.3
  277.4 2.5 final.3
  (27 shorter events, 1.2 us)
Async XLA Ops:
  7.2 156.2 %all-gather.3.cloned.1.call-start = ((), (), s32[]{:S(2)}) async-start(), calls=%async_computation.2 | async-start | bytes 14155776 | tf_op jit(solution)/shard_map/all_gather | solution.py:338
  15.8 66.5 %all-to-all-start = ((bf16[32,544,128]{2,1,0:T(8,128)(2,1)}), bf16[32,544,128]{2,1,0:T(8,128)(2,1)}, u32[]{:S(2)}, u32[]{:S(2)}) async-start(bf16[32,544,128]{2,1,0:T(8,128)(2,1)} %dispatch.2), calls=%async_computation | async-start | bytes 8912896 | tf_op jit(solution)/shard_map/all_to_all | solution.py:336
  82.3 61.6 %all-to-all-start.1 = ((bf16[32,544,128]{2,1,0:T(8,128)(2,1)}), bf16[32,544,128]{2,1,0:T(8,128)(2,1)}, u32[]{:S(2)}, u32[]{:S(2)}) async-start(bf16[32,544,128]{2,1,0:T(8,128)(2,1)} %dispatch.3), calls=%async_computation.1 | async-start | bytes 8912896 | tf_op jit(solution)/shard_map/all_to_all | solution.py:336
  107.4 50.7 %collective-permute-start = (bf16[192,2048]{1,0:T(8,128)(2,1)}, bf16[192,2048]{1,0:T(8,128)(2,1)S(1)}, u32[]{:S(2)}, u32[]{:S(2)}) collective-permute-start(bf16[192,2048]{1,0:T(8,128)(2,1)} %get-tuple-element.94), channel_id=1, source_target_pairs={{0,32},{1,225},{2,34},{3,227},{4,36},{5,229},{6,38},{7,231},{8,40}... | collective-permute-start | bytes 2359304 | tf_op jit(solution)/shard_map/ppermute | solution.py:321
  156.1 16.0 %collective-permute-start.2 = (bf16[192,2048]{1,0:T(8,128)(2,1)}, bf16[192,2048]{1,0:T(8,128)(2,1)S(1)}, u32[]{:S(2)}, u32[]{:S(2)}) collective-permute-start(bf16[192,2048]{1,0:T(8,128)(2,1)} %get-tuple-element.104), channel_id=1, source_target_pairs={{0,32},{1,225},{2,34},{3,227},{4,36},{5,229},{6,38},{7,231},{8,40}... | collective-permute-start | bytes 2359304 | tf_op jit(solution)/shard_map/ppermute | solution.py:321
  158.0 0.9 copy-start.2
  158.9 21.8 %slice-start = ((s8[6291456]{0:T(1024)(128)(4,1)}), s8[2097152]{0:T(1024)(128)(4,1)S(1)}, s32[]{:S(2)}) async-start(s8[6291456]{0:T(1024)(128)(4,1)} %bitcast.36), calls=%async_computation.3 | async-start | bytes 4194304
  161.4 19.3 %collective-permute-start.1 = (bf16[192,2048]{1,0:T(8,128)(2,1)}, bf16[192,2048]{1,0:T(8,128)(2,1)}, u32[]{:S(2)}, u32[]{:S(2)}) collective-permute-start(bf16[192,2048]{1,0:T(8,128)(2,1)} %bitcast_add_fusion.11), channel_id=1, source_target_pairs={{0,32},{1,225},{2,34},{3,227},{4,36},{5,229},{6,38},{7,231},{8,40}... | collective-permute-start | bytes 2359304 | tf_op jit(solution)/shard_map/ppermute | solution.py:321
  163.3 17.4 %slice-start.1 = ((s8[6291456]{0:T(1024)(128)(4,1)}), s8[4194304]{0:T(1024)(128)(4,1)S(1)}, s32[]{:S(2)}) async-start(s8[6291456]{0:T(1024)(128)(4,1)} %bitcast.36), calls=%async_computation.4 | async-start | bytes 8388608
  174.2 15.2 %collective-permute-start.4 = (bf16[192,2048]{1,0:T(8,128)(2,1)}, bf16[192,2048]{1,0:T(8,128)(2,1)}, u32[]{:S(2)}, u32[]{:S(2)}) collective-permute-start(bf16[192,2048]{1,0:T(8,128)(2,1)} %bitcast_add_fusion.10), channel_id=1, source_target_pairs={{0,32},{1,225},{2,34},{3,227},{4,36},{5,229},{6,38},{7,231},{8,40}... | collective-permute-start | bytes 2359304 | tf_op jit(solution)/shard_map/ppermute | solution.py:321
  182.8 14.7 %collective-permute-start.3 = (bf16[192,2048]{1,0:T(8,128)(2,1)}, bf16[192,2048]{1,0:T(8,128)(2,1)}, u32[]{:S(2)}, u32[]{:S(2)}) collective-permute-start(bf16[192,2048]{1,0:T(8,128)(2,1)} %bitcast_add_fusion.9), channel_id=1, source_target_pairs={{0,32},{1,225},{2,34},{3,227},{4,36},{5,229},{6,38},{7,231},{8,40}... | collective-permute-start | bytes 2359304 | tf_op jit(solution)/shard_map/ppermute | solution.py:321
  190.9 15.1 %collective-permute-start.6 = (bf16[192,2048]{1,0:T(8,128)(2,1)S(1)}, bf16[192,2048]{1,0:T(8,128)(2,1)}, u32[]{:S(2)}, u32[]{:S(2)}) collective-permute-start(bf16[192,2048]{1,0:T(8,128)(2,1)S(1)} %bitcast_add_fusion.8), channel_id=1, source_target_pairs={{0,32},{1,225},{2,34},{3,227},{4,36},{5,229},{6,38},{7,231},{8,40}... | collective-permute-start | bytes 2359304 | tf_op jit(solution)/shard_map/ppermute | solution.py:321
  199.6 14.7 %collective-permute-start.5 = (bf16[192,2048]{1,0:T(8,128)(2,1)}, bf16[192,2048]{1,0:T(8,128)(2,1)}, u32[]{:S(2)}, u32[]{:S(2)}) collective-permute-start(bf16[192,2048]{1,0:T(8,128)(2,1)} %bitcast_add_fusion.7), channel_id=1, source_target_pairs={{0,32},{1,225},{2,34},{3,227},{4,36},{5,229},{6,38},{7,231},{8,40}... | collective-permute-start | bytes 2359304 | tf_op jit(solution)/shard_map/ppermute | solution.py:321
  207.4 15.4 %collective-permute-start.8 = (bf16[192,2048]{1,0:T(8,128)(2,1)S(1)}, bf16[192,2048]{1,0:T(8,128)(2,1)}, u32[]{:S(2)}, u32[]{:S(2)}) collective-permute-start(bf16[192,2048]{1,0:T(8,128)(2,1)S(1)} %bitcast_add_fusion.6), channel_id=1, source_target_pairs={{0,32},{1,225},{2,34},{3,227},{4,36},{5,229},{6,38},{7,231},{8,40}... | collective-permute-start | bytes 2359304 | tf_op jit(solution)/shard_map/ppermute | solution.py:321
  216.5 14.7 %collective-permute-start.7 = (bf16[192,2048]{1,0:T(8,128)(2,1)}, bf16[192,2048]{1,0:T(8,128)(2,1)}, u32[]{:S(2)}, u32[]{:S(2)}) collective-permute-start(bf16[192,2048]{1,0:T(8,128)(2,1)} %bitcast_add_fusion.5), channel_id=1, source_target_pairs={{0,32},{1,225},{2,34},{3,227},{4,36},{5,229},{6,38},{7,231},{8,40}... | collective-permute-start | bytes 2359304 | tf_op jit(solution)/shard_map/ppermute | solution.py:321
  224.3 15.7 %collective-permute-start.10 = (bf16[192,2048]{1,0:T(8,128)(2,1)S(1)}, bf16[192,2048]{1,0:T(8,128)(2,1)}, u32[]{:S(2)}, u32[]{:S(2)}) collective-permute-start(bf16[192,2048]{1,0:T(8,128)(2,1)S(1)} %bitcast_add_fusion.4), channel_id=1, source_target_pairs={{0,32},{1,225},{2,34},{3,227},{4,36},{5,229},{6,38},{7,231},{8,40}... | collective-permute-start | bytes 2359304 | tf_op jit(solution)/shard_map/ppermute | solution.py:321
  233.4 14.7 %collective-permute-start.9 = (bf16[192,2048]{1,0:T(8,128)(2,1)}, bf16[192,2048]{1,0:T(8,128)(2,1)}, u32[]{:S(2)}, u32[]{:S(2)}) collective-permute-start(bf16[192,2048]{1,0:T(8,128)(2,1)} %bitcast_add_fusion.3), channel_id=1, source_target_pairs={{0,32},{1,225},{2,34},{3,227},{4,36},{5,229},{6,38},{7,231},{8,40}... | collective-permute-start | bytes 2359304 | tf_op jit(solution)/shard_map/ppermute | solution.py:321
  241.4 15.1 %collective-permute-start.11 = (bf16[192,2048]{1,0:T(8,128)(2,1)S(1)}, bf16[192,2048]{1,0:T(8,128)(2,1)}, u32[]{:S(2)}, u32[]{:S(2)}) collective-permute-start(bf16[192,2048]{1,0:T(8,128)(2,1)S(1)} %bitcast_add_fusion.2), channel_id=1, source_target_pairs={{0,32},{1,225},{2,34},{3,227},{4,36},{5,229},{6,38},{7,231},{8,40}... | collective-permute-start | bytes 2359304 | tf_op jit(solution)/shard_map/ppermute | solution.py:321
  250.2 4.7 %copy-start.1 = (bf16[192,2048]{1,0:T(8,128)(2,1)S(1)}, bf16[192,2048]{1,0:T(8,128)(2,1)}, u32[]{:S(2)}) copy-start(bf16[192,2048]{1,0:T(8,128)(2,1)} %bitcast_add_fusion.1) | copy-start | bytes 2359300
  254.8 13.2 %collective-permute-start.13 = (bf16[192,2048]{1,0:T(8,128)(2,1)S(1)}, bf16[192,2048]{1,0:T(8,128)(2,1)S(1)}, u32[]{:S(2)}, u32[]{:S(2)}) collective-permute-start(bf16[192,2048]{1,0:T(8,128)(2,1)S(1)} %copy-done.1), channel_id=1, source_target_pairs={{0,32},{1,225},{2,34},{3,227},{4,36},{5,229},{6,38},{7,231},{8,40}... | collective-permute-start | bytes 2359304 | tf_op jit(solution)/shard_map/ppermute | solution.py:321
  258.0 18.5 %collective-permute-start.12 = (bf16[192,2048]{1,0:T(8,128)(2,1)S(1)}, bf16[192,2048]{1,0:T(8,128)(2,1)S(1)}, u32[]{:S(2)}, u32[]{:S(2)}) collective-permute-start(bf16[192,2048]{1,0:T(8,128)(2,1)S(1)} %bitcast_add_fusion), channel_id=1, source_target_pairs={{0,32},{1,225},{2,34},{3,227},{4,36},{5,229},{6,38},{7,231},{8,40}... | collective-permute-start | bytes 2359304 | tf_op jit(solution)/shard_map/ppermute | solution.py:321
  268.0 0.9 copy-start
  276.5 0.9 copy-start.3
Sparse Core Ops, SparseCore 0:
  10.8 144.7 all-gather.2

commit v3 on v2

--- a/solution.py
+++ b/solution.py
@@ -25,7 +25,8 @@
     return lax.broadcasted_iota(jnp.int32, shape, dim)
 
 
-def dispatch_kernel(ids_ref, gates_ref, grad_ref, out_ref, main_ref, tail_ref):
+def dispatch_kernel(ids_ref, gates_ref, grad_ref, *refs):
+    out_ref, main_ref, tail_ref = refs[-3:]
     top, tokens = ids_ref.shape
     dests = out_ref.shape[0]
     experts = 2 * dests
@@ -62,7 +63,7 @@
     out_ref[:, 2 * MAIN * FOLD :, :] = rows.reshape(dests, 2 * FOLD, LANE)
 
 
-def dispatch(ids, gates, grad, dests, first, count):
+def dispatch(ids, gates, grad, dests, first, count, after=()):
     tokens, _ = grad.shape
     ids, gates = jnp.transpose(ids), jnp.transpose(gates)
     return pl.pallas_call(
@@ -72,7 +73,8 @@
             pl.BlockSpec(ids.shape, lambda i: (0, 0)),
             pl.BlockSpec(gates.shape, lambda i: (0, 0)),
             pl.BlockSpec((tokens, WIDE), lambda i: (0, first + i)),
-        ],
+        ]
+        + [pl.BlockSpec(memory_space=pl.ANY)] * len(after),
         out_specs=pl.BlockSpec((dests, BLOCK, LANE), lambda i: (0, i, 0)),
         out_shape=jax.ShapeDtypeStruct((dests, count * BLOCK, LANE), BF),
         scratch_shapes=[
@@ -84,7 +86,7 @@
             flops=count * 2 * 1088 * 128 * WIDE, bytes_accessed=count * 3 << 20, transcendentals=0
         ),
         name="dispatch",
-    )(ids, gates, grad)
+    )(ids, gates, grad, *after)
 
 
 def natural(order, sources):
@@ -336,14 +338,17 @@
         return lax.all_to_all(rows, "expert", split_axis=0, concat_axis=0, tiled=True)
 
     weights = lax.all_gather(jnp.transpose(down_weight, (1, 0, 2)), "dp", axis=0, tiled=False)
-    arrived = [exchange(dispatch(expert_ids, gate_weights, grad_out, sources, at, 2)) for at in (0, 2)]
+    first = exchange(dispatch(expert_ids, gate_weights, grad_out, sources, 0, 2))
     hidden, gate, up = arrange(saved_gate, saved_up, sources)
+    second = exchange(dispatch(expert_ids, gate_weights, grad_out, sources, 2, 2, (hidden,)))
 
     slots, rings, total = [], [], [(), ()]
-    for half in range(2):
-        rows, rest, sent = partial_down(place, clock(arrived[half]), hidden, groups, 0, 2)
+    for arrived in (first, second):
+        rows, rest, sent = partial_down(place, clock(arrived), hidden, groups, 0, 2)
         slots.append(rows)
         rings.append(Ring(clock, rest, clock(sent)))
+        if len(rings) == 1:
+            rings[0].step()
 
     def hidden_piece(half, e):
         piece = hidden_grad(clock.value, [slots[half]], weights, half, e, total[e])
@@ -354,7 +359,8 @@
 
     grads = ()
     for turn in range(1, groups - 1):
-        rings[0].step()
+        if rings[0].turn < groups - 2:
+            rings[0].step()
         if turn in (1, 2, 4, 5):
             hidden_piece((turn - 1) % 3, turn // 3)
         else:

time: 288 us -> 282 us (0.979)
    all_to_all x2, waiting for transfers between devices: 88.4 us -> 56.2 us  [exchange(): lax.all_to_all(rows, 'expert', split_axis=0, concat_axis=0, tiled=True)]
    ppermute x14, waiting for transfers between devices: 53.1 us -> 83.9 us  [send(): self.got = lax.ppermute(blocks, ('dp', 'expert'), self.pairs)]
    unnamed x13 -> x9, local copies, waits for them, and re-layouts: 6.14 us -> 5.24 us
  transfers between devices with their start and end apart: 17 -> 17, of which waited for: 13 -> 14; matrix products, arithmetic and copies ran while one was open for 8% -> 7% of each run, Pallas kernels for 28% -> 28%
where the time goes in v3:
time: 282 us; the launch traced here: 281 us
  waiting for transfers between devices  140 us (50%)
  Pallas kernels  81.7 us (29%)
  other arithmetic  21.9 us (8%)
  starting transfers between devices  18.3 us (6%)
  between operations  14.1 us (5%)
  local copies, waits for them, and re-layouts  5.24 us (2%)
    ppermute x14, waiting for transfers between devices, send(): self.got = lax.ppermute(blocks, ('dp', 'expert'), self.pairs)  83.9 us
    all_to_all x2, waiting for transfers between devices, exchange(): lax.all_to_all(rows, 'expert', split_axis=0, concat_axis=0, tiled=True)  56.2 us
    pallas_call x4, Pallas kernels, hidden_grad(): pl.pallas_call(functools.partial(hidden_grad_kernel, count), grid=(each *...  25.4 us
    pallas_call x2, Pallas kernels, partial_down(): pl.pallas_call(down_kernel, grid=(count, 2), in_specs=[pl.BlockSpec(memor...  24.5 us
    add x12, other arithmetic, step(): self.send(self.clock(self.clock(self.got) + self.rest[self.turn]))  21.2 us
    all_to_all x2, starting transfers between devices, exchange(): lax.all_to_all(rows, 'expert', split_axis=0, concat_axis=0, tiled=True)  12.2 us
    pallas_call x2, Pallas kernels, dispatch(): pl.pallas_call(dispatch_kernel, grid=(count,), in_specs=[pl.BlockSpec(ids...  10.1 us
    pallas_call x2, Pallas kernels, gate_grads(): pl.pallas_call(functools.partial(gate_grads_kernel, sources), grid=(1,),...  9.17 us
  transfers between devices with their start and end apart: 17, of which 14 were waited for; matrix products, arithmetic and copies ran while one was open for 7% of the time, Pallas kernels for 28%

profile of v3, /device:TPU:8, one launch (start us, length us, event | category | flops | bytes accessed | tf_op | source)
XLA Modules:
  0.0 281.4 jit_solution(2423192529179084760)
XLA Ops:
  7.2 3.4 %copy.15 = bf16[96,2,4096]{2,0,1:T(8,128)(2,1)} copy(bf16[96,2,4096]{2,1,0:T(2,128)(2,1)} %param.11) | data formatting | bytes 3145728 | tf_op args[5]
  10.7 5.1 %dispatch.3 = bf16[32,544,128]{2,1,0:T(8,128)(2,1)} custom-call(s32[8,128]{1,0:T(8,128)} %bitcast.39, bf16[8,128]{1,0:T(8,128)(2,1)} %bitcast.41, bf16[128,4096]{1,0:T(8,128)(2,1)} %grad_ref.3), custom_call_target="tpu_custom_call" | custom-call | flops 570425344 | bytes 6291456 | tf_op jit(solution)/shard_map/dispatch/pallas_call | solution.py:69
  15.7 7.6 %all-to-all-start.1 = ((bf16[32,544,128]{2,1,0:T(8,128)(2,1)}), bf16[32,544,128]{2,1,0:T(8,128)(2,1)}, u32[]{:S(2)}, u32[]{:S(2)}) async-start(bf16[32,544,128]{2,1,0:T(8,128)(2,1)} %dispatch.3), calls=%async_computation.1 | async-start | bytes 8912896 | tf_op jit(solution)/shard_map/all_to_all | solution.py:338
  23.3 7.5 %arrange.1 = (bf16[2,768,544]{2,1,0:T(8,128)(2,1)}, bf16[2,544,768]{2,1,0:T(8,128)(2,1)}, bf16[2,544,768]{2,1,0:T(8,128)(2,1)}) custom-call(bf16[2,544,768]{2,1,0:T(8,128)(2,1)} %gate_ref.1, bf16[2,544,768]{2,1,0:T(8,128)(2,1)} %up_ref.1), custom_call_target="tpu_custom_call" | custom-call | flops 2727346176 | bytes 9437184 | tf_op jit(solution)/shard_map/arrange/pallas_call | solution.py:113
  30.8 5.0 %dispatch.2 = bf16[32,544,128]{2,1,0:T(8,128)(2,1)} custom-call(s32[8,128]{1,0:T(8,128)} %bitcast.40, bf16[8,128]{1,0:T(8,128)(2,1)} %bitcast.42, bf16[128,4096]{1,0:T(8,128)(2,1)} %grad_ref.3, bf16[2,768,544]{2,1,0:T(8,128)(2,1)} %get-tuple-element.90.refs_0_.hidden_ref), custom_call_target="tpu_custom_call" | custom-call | flops 570425344 | bytes 6291456 | tf_op jit(solution)/shard_map/dispatch/pallas_call | solution.py:69
  35.9 46.4 %all-to-all-done.1.rows_ref = bf16[32,544,128]{2,1,0:T(8,128)(2,1)} async-done(((bf16[32,544,128]{2,1,0:T(8,128)(2,1)}), bf16[32,544,128]{2,1,0:T(8,128)(2,1)}, u32[]{:S(2)}, u32[]{:S(2)}) %all-to-all-start.1) | async-done | bytes 4456480 | tf_op jit(solution)/shard_map/all_to_all | solution.py:338
  82.2 4.7 %all-to-all-start = ((bf16[32,544,128]{2,1,0:T(8,128)(2,1)}), bf16[32,544,128]{2,1,0:T(8,128)(2,1)}, u32[]{:S(2)}, u32[]{:S(2)}) async-start(bf16[32,544,128]{2,1,0:T(8,128)(2,1)} %dispatch.2), calls=%async_computation | async-start | bytes 8912896 | tf_op jit(solution)/shard_map/all_to_all | solution.py:338
  86.9 0.7 pad_add_fusion.place_ref.refs_0_.after_ref
  87.6 12.3 %partial_down.2 = (bf16[2,544,2048]{2,1,0:T(8,128)(2,1)}, bf16[8,192,2048]{2,1,0:T(8,128)(2,1)}, bf16[192,2048]{1,0:T(8,128)(2,1)}) custom-call(s32[2]{0:T(128)} %pad_add_fusion.place_ref.refs_0_.after_ref, bf16[32,544,128]{2,1,0:T(8,128)(2,1)} %all-to-all-done.1.rows_ref, bf16[2,768,544]{2,1,0:T(8,128)(2,1)} %get-tuple-element.90.refs_0_.hidden_ref), custom_call_target="tpu_custom_call" | custom-call | flops 3422552064 | bytes 18874368 | tf_op jit(solution)/shard_map/partial_down/pallas_call | solution.py:164
  99.9 1.9 collective-permute-start
  101.7 31.0 %collective-permute-done = bf16[192,2048]{1,0:T(8,128)(2,1)S(1)} collective-permute-done((bf16[192,2048]{1,0:T(8,128)(2,1)}, bf16[192,2048]{1,0:T(8,128)(2,1)S(1)}, u32[]{:S(2)}, u32[]{:S(2)}) %collective-permute-start) | collective-permute-done | bytes 786464 | tf_op jit(solution)/shard_map/ppermute | solution.py:323
  132.7 1.2 bitcast_add_fusion.11
  134.0 9.8 %all-to-all-done.rows_ref = bf16[32,544,128]{2,1,0:T(8,128)(2,1)} async-done(((bf16[32,544,128]{2,1,0:T(8,128)(2,1)}), bf16[32,544,128]{2,1,0:T(8,128)(2,1)}, u32[]{:S(2)}, u32[]{:S(2)}) %all-to-all-start) | async-done | bytes 4456480 | tf_op jit(solution)/shard_map/all_to_all | solution.py:338
  143.8 12.2 %partial_down.3 = (bf16[2,544,2048]{2,1,0:T(8,128)(2,1)}, bf16[8,192,2048]{2,1,0:T(8,128)(2,1)}, bf16[192,2048]{1,0:T(8,128)(2,1)}) custom-call(s32[2]{0:T(128)} %pad_add_fusion.place_ref.refs_0_.after_ref, bf16[32,544,128]{2,1,0:T(8,128)(2,1)} %all-to-all-done.rows_ref, bf16[2,768,544]{2,1,0:T(8,128)(2,1)} %get-tuple-element.90.refs_0_.hidden_ref), custom_call_target="tpu_custom_call" | custom-call | flops 3422552064 | bytes 18874368 | tf_op jit(solution)/shard_map/partial_down/pallas_call | solution.py:164
  156.1 1.9 collective-permute-start.1
  158.0 5.5 %collective-permute-done.2 = bf16[192,2048]{1,0:T(8,128)(2,1)} collective-permute-done((bf16[192,2048]{1,0:T(8,128)(2,1)S(1)}, bf16[192,2048]{1,0:T(8,128)(2,1)}, u32[]{:S(2)}, u32[]{:S(2)}) %collective-permute-start.2) | collective-permute-done | bytes 786464 | tf_op jit(solution)/shard_map/ppermute | solution.py:323
  163.5 2.5 bitcast_add_fusion.10
  166.0 6.2 %hidden_grad.4.refs_2_ = f32[544,768]{1,0:T(8,128)} custom-call(s32[2]{0:T(128)} %pad_add_fusion.place_ref.refs_0_.after_ref, bf16[2,544,2048]{2,1,0:T(8,128)(2,1)} %get-tuple-element.109.refs_1_, bf16[8,2,96,4096]{3,2,1,0:T(8,128)(2,1)} %bitcast.32), custom_call_target="tpu_custom_call" | custom-call | flops 1711276032 | bytes 9437184 | tf_op jit(solution)/shard_map/hidden_grad/pallas_call | solution.py:221
  172.2 2.1 bitcast_add_fusion.9
  174.3 6.3 %collective-permute-done.4 = bf16[192,2048]{1,0:T(8,128)(2,1)} collective-permute-done((bf16[192,2048]{1,0:T(8,128)(2,1)}, bf16[192,2048]{1,0:T(8,128)(2,1)}, u32[]{:S(2)}, u32[]{:S(2)}) %collective-permute-start.4) | collective-permute-done | bytes 786464 | tf_op jit(solution)/shard_map/ppermute | solution.py:323
  180.6 2.1 bitcast_add_fusion.8
  182.7 6.6 %hidden_grad.5.total_ref = f32[544,768]{1,0:T(8,128)} custom-call(s32[2]{0:T(128)} %pad_add_fusion.place_ref.refs_0_.after_ref, bf16[2,544,2048]{2,1,0:T(8,128)(2,1)} %get-tuple-element.120.refs_1_, f32[544,768]{1,0:T(8,128)} %hidden_grad.4.refs_2_, bf16[8,2,96,4096]{3,2,1,0:T(8,128)(2,1)} %bitcast.33), custom_call_target="tpu_custom_call" | custom-call | flops 1711276032 | bytes 9437184 | tf_op jit(solution)/shard_map/hidden_grad/pallas_call | solution.py:221
  189.3 1.5 bitcast_add_fusion.7
  190.9 6.6 %collective-permute-done.6 = bf16[192,2048]{1,0:T(8,128)(2,1)} collective-permute-done((bf16[192,2048]{1,0:T(8,128)(2,1)}, bf16[192,2048]{1,0:T(8,128)(2,1)}, u32[]{:S(2)}, u32[]{:S(2)}) %collective-permute-start.6) | collective-permute-done | bytes 786464 | tf_op jit(solution)/shard_map/ppermute | solution.py:323
  197.5 2.1 bitcast_add_fusion.6
  199.6 4.6 %gate_grads.2 = (bf16[2,544,768]{2,1,0:T(8,128)(2,1)}, bf16[2,544,768]{2,1,0:T(8,128)(2,1)}) custom-call(s32[2]{0:T(128)} %pad_add_fusion.place_ref.refs_0_.after_ref, f32[544,768]{1,0:T(8,128)} %hidden_grad.5.total_ref, bf16[2,544,768]{2,1,0:T(8,128)(2,1)} %get-tuple-element.132.gate_ref, bf16[2,544,768]{2,1,0:T(8,128)(2,1)} %get-tuple-element.133.up_ref), custom_call_target="tpu_custom_call" | custom-call | flops 909115392 | bytes 5242880 | tf_op jit(solution)/shard_map/gate_grads/pallas_call | solution.py:255
  204.2 1.7 collective-permute-done.5
  205.9 1.5 bitcast_add_fusion.5
  207.4 6.9 %collective-permute-done.8 = bf16[192,2048]{1,0:T(8,128)(2,1)} collective-permute-done((bf16[192,2048]{1,0:T(8,128)(2,1)}, bf16[192,2048]{1,0:T(8,128)(2,1)}, u32[]{:S(2)}, u32[]{:S(2)}) %collective-permute-start.8) | collective-permute-done | bytes 786464 | tf_op jit(solution)/shard_map/ppermute | solution.py:323
  214.3 2.1 bitcast_add_fusion.4
  216.4 6.0 %hidden_grad.6.refs_2_ = f32[544,768]{1,0:T(8,128)} custom-call(s32[2]{0:T(128)} %pad_add_fusion.place_ref.refs_0_.after_ref, bf16[2,544,2048]{2,1,0:T(8,128)(2,1)} %get-tuple-element.109.refs_1_, bf16[8,2,96,4096]{3,2,1,0:T(8,128)(2,1)} %bitcast.34), custom_call_target="tpu_custom_call" | custom-call | flops 1711276032 | bytes 9437184 | tf_op jit(solution)/shard_map/hidden_grad/pallas_call | solution.py:221
  222.7 2.4 bitcast_add_fusion.3
  225.1 0.5 collective-permute-start.9
  225.6 5.5 %collective-permute-done.10 = bf16[192,2048]{1,0:T(8,128)(2,1)} collective-permute-done((bf16[192,2048]{1,0:T(8,128)(2,1)}, bf16[192,2048]{1,0:T(8,128)(2,1)}, u32[]{:S(2)}, u32[]{:S(2)}) %collective-permute-start.10) | collective-permute-done | bytes 786464 | tf_op jit(solution)/shard_map/ppermute | solution.py:323
  231.2 1.2 bitcast_add_fusion.2
  232.4 6.6 %hidden_grad.7.total_ref = f32[544,768]{1,0:T(8,128)} custom-call(s32[2]{0:T(128)} %pad_add_fusion.place_ref.refs_0_.after_ref, bf16[2,544,2048]{2,1,0:T(8,128)(2,1)} %get-tuple-element.120.refs_1_, f32[544,768]{1,0:T(8,128)} %hidden_grad.6.refs_2_, bf16[8,2,96,4096]{3,2,1,0:T(8,128)(2,1)} %bitcast.35), custom_call_target="tpu_custom_call" | custom-call | flops 1711276032 | bytes 9437184 | tf_op jit(solution)/shard_map/hidden_grad/pallas_call | solution.py:221
  239.0 0.6 collective-permute-done.9
  239.6 1.5 bitcast_add_fusion.1
  241.1 1.3 collective-permute-start.13
  242.5 4.6 %gate_grads.3 = (bf16[2,544,768]{2,1,0:T(8,128)(2,1)}, bf16[2,544,768]{2,1,0:T(8,128)(2,1)}) custom-call(s32[2]{0:T(128)} %pad_add_fusion.place_ref.refs_0_.after_ref, f32[544,768]{1,0:T(8,128)} %hidden_grad.7.total_ref, bf16[2,544,768]{2,1,0:T(8,128)(2,1)} %get-tuple-element.132.gate_ref, ...), custom_call_target="tpu_custom_call", output_to_operand_aliasing={{0}: (4, {}), {1}: (5, {})} | custom-call | flops 909115392 | bytes 5242880 | tf_op jit(solution)/shard_map/gate_grads/pallas_call | solution.py:255
  247.0 7.3 %collective-permute-done.11 = bf16[192,2048]{1,0:T(8,128)(2,1)S(1)} collective-permute-done((bf16[192,2048]{1,0:T(8,128)(2,1)S(1)}, bf16[192,2048]{1,0:T(8,128)(2,1)S(1)}, u32[]{:S(2)}, u32[]{:S(2)}) %collective-permute-start.11) | collective-permute-done | bytes 786464 | tf_op jit(solution)/shard_map/ppermute | solution.py:323
  254.3 1.2 bitcast_add_fusion
  255.6 7.1 %collective-permute-done.13.arrived_ref = bf16[192,2048]{1,0:T(8,128)(2,1)S(1)} collective-permute-done((bf16[192,2048]{1,0:T(8,128)(2,1)S(1)}, bf16[192,2048]{1,0:T(8,128)(2,1)S(1)}, u32[]{:S(2)}, u32[]{:S(2)}) %collective-permute-start.13) | collective-permute-done | bytes 786464 | tf_op jit(solution)/shard_map/ppermute | solution.py:323
  262.8 0.9 copy-done
  263.7 2.5 final.2.refs_0_
  266.1 5.1 %collective-permute-done.12.arrived_ref = bf16[192,2048]{1,0:T(8,128)(2,1)S(1)} collective-permute-done((bf16[192,2048]{1,0:T(8,128)(2,1)S(1)}, bf16[192,2048]{1,0:T(8,128)(2,1)S(1)}, u32[]{:S(2)}, u32[]{:S(2)}) %collective-permute-start.12) | collective-permute-done | bytes 786464 | tf_op jit(solution)/shard_map/ppermute | solution.py:323
  271.2 0.9 copy-done.1
  272.1 2.5 final.3
  (23 shorter events, 0.8 us)
Async XLA Ops:
  7.2 158.8 %all-gather.3.cloned.1.call-start = ((), (), s32[]{:S(2)}) async-start(), calls=%async_computation.2 | async-start | bytes 14155776 | tf_op jit(solution)/shard_map/all_gather | solution.py:340
  15.7 66.5 %all-to-all-start.1 = ((bf16[32,544,128]{2,1,0:T(8,128)(2,1)}), bf16[32,544,128]{2,1,0:T(8,128)(2,1)}, u32[]{:S(2)}, u32[]{:S(2)}) async-start(bf16[32,544,128]{2,1,0:T(8,128)(2,1)} %dispatch.3), calls=%async_computation.1 | async-start | bytes 8912896 | tf_op jit(solution)/shard_map/all_to_all | solution.py:338
  82.2 61.6 %all-to-all-start = ((bf16[32,544,128]{2,1,0:T(8,128)(2,1)}), bf16[32,544,128]{2,1,0:T(8,128)(2,1)}, u32[]{:S(2)}, u32[]{:S(2)}) async-start(bf16[32,544,128]{2,1,0:T(8,128)(2,1)} %dispatch.2), calls=%async_computation | async-start | bytes 8912896 | tf_op jit(solution)/shard_map/all_to_all | solution.py:338
  99.9 32.9 %collective-permute-start = (bf16[192,2048]{1,0:T(8,128)(2,1)}, bf16[192,2048]{1,0:T(8,128)(2,1)S(1)}, u32[]{:S(2)}, u32[]{:S(2)}) collective-permute-start(bf16[192,2048]{1,0:T(8,128)(2,1)} %get-tuple-element.94), channel_id=1, source_target_pairs={{0,32},{1,225},{2,34},{3,227},{4,36},{5,229},{6,38},{7,231},{8,40}... | collective-permute-start | bytes 2359304 | tf_op jit(solution)/shard_map/ppermute | solution.py:323
  133.9 29.6 %collective-permute-start.2 = (bf16[192,2048]{1,0:T(8,128)(2,1)S(1)}, bf16[192,2048]{1,0:T(8,128)(2,1)}, u32[]{:S(2)}, u32[]{:S(2)}) collective-permute-start(bf16[192,2048]{1,0:T(8,128)(2,1)S(1)} %bitcast_add_fusion.11), channel_id=1, source_target_pairs={{0,32},{1,225},{2,34},{3,227},{4,36},{5,229},{6,38},{7,231},{8,40}... | collective-permute-start | bytes 2359304 | tf_op jit(solution)/shard_map/ppermute | solution.py:323
  156.1 16.1 %collective-permute-start.1 = (bf16[192,2048]{1,0:T(8,128)(2,1)}, bf16[192,2048]{1,0:T(8,128)(2,1)S(1)}, u32[]{:S(2)}, u32[]{:S(2)}) collective-permute-start(bf16[192,2048]{1,0:T(8,128)(2,1)} %get-tuple-element.103), channel_id=1, source_target_pairs={{0,32},{1,225},{2,34},{3,227},{4,36},{5,229},{6,38},{7,231},{8,40}... | collective-permute-start | bytes 2359304 | tf_op jit(solution)/shard_map/ppermute | solution.py:323
  163.5 17.1 %slice-start = ((s8[6291456]{0:T(1024)(128)(4,1)}), s8[2097152]{0:T(1024)(128)(4,1)S(1)}, s32[]{:S(2)}) async-start(s8[6291456]{0:T(1024)(128)(4,1)} %bitcast.36), calls=%async_computation.3 | async-start | bytes 4194304
  166.0 14.6 %collective-permute-start.4 = (bf16[192,2048]{1,0:T(8,128)(2,1)}, bf16[192,2048]{1,0:T(8,128)(2,1)}, u32[]{:S(2)}, u32[]{:S(2)}) collective-permute-start(bf16[192,2048]{1,0:T(8,128)(2,1)} %bitcast_add_fusion.10), channel_id=1, source_target_pairs={{0,32},{1,225},{2,34},{3,227},{4,36},{5,229},{6,38},{7,231},{8,40}... | collective-permute-start | bytes 2359304 | tf_op jit(solution)/shard_map/ppermute | solution.py:323
  166.0 14.6 %slice-start.1 = ((s8[6291456]{0:T(1024)(128)(4,1)}), s8[4194304]{0:T(1024)(128)(4,1)S(1)}, s32[]{:S(2)}) async-start(s8[6291456]{0:T(1024)(128)(4,1)} %bitcast.36), calls=%async_computation.4 | async-start | bytes 8388608
  174.3 15.1 %collective-permute-start.3 = (bf16[192,2048]{1,0:T(8,128)(2,1)}, bf16[192,2048]{1,0:T(8,128)(2,1)}, u32[]{:S(2)}, u32[]{:S(2)}) collective-permute-start(bf16[192,2048]{1,0:T(8,128)(2,1)} %bitcast_add_fusion.9), channel_id=1, source_target_pairs={{0,32},{1,225},{2,34},{3,227},{4,36},{5,229},{6,38},{7,231},{8,40}... | collective-permute-start | bytes 2359304 | tf_op jit(solution)/shard_map/ppermute | solution.py:323
  182.7 14.7 %collective-permute-start.6 = (bf16[192,2048]{1,0:T(8,128)(2,1)}, bf16[192,2048]{1,0:T(8,128)(2,1)}, u32[]{:S(2)}, u32[]{:S(2)}) collective-permute-start(bf16[192,2048]{1,0:T(8,128)(2,1)} %bitcast_add_fusion.8), channel_id=1, source_target_pairs={{0,32},{1,225},{2,34},{3,227},{4,36},{5,229},{6,38},{7,231},{8,40}... | collective-permute-start | bytes 2359304 | tf_op jit(solution)/shard_map/ppermute | solution.py:323
  190.8 15.1 %collective-permute-start.5 = (bf16[192,2048]{1,0:T(8,128)(2,1)S(1)}, bf16[192,2048]{1,0:T(8,128)(2,1)}, u32[]{:S(2)}, u32[]{:S(2)}) collective-permute-start(bf16[192,2048]{1,0:T(8,128)(2,1)S(1)} %bitcast_add_fusion.7), channel_id=1, source_target_pairs={{0,32},{1,225},{2,34},{3,227},{4,36},{5,229},{6,38},{7,231},{8,40}... | collective-permute-start | bytes 2359304 | tf_op jit(solution)/shard_map/ppermute | solution.py:323
  199.6 14.7 %collective-permute-start.8 = (bf16[192,2048]{1,0:T(8,128)(2,1)}, bf16[192,2048]{1,0:T(8,128)(2,1)}, u32[]{:S(2)}, u32[]{:S(2)}) collective-permute-start(bf16[192,2048]{1,0:T(8,128)(2,1)} %bitcast_add_fusion.6), channel_id=1, source_target_pairs={{0,32},{1,225},{2,34},{3,227},{4,36},{5,229},{6,38},{7,231},{8,40}... | collective-permute-start | bytes 2359304 | tf_op jit(solution)/shard_map/ppermute | solution.py:323
  207.3 15.4 %collective-permute-start.7 = (bf16[192,2048]{1,0:T(8,128)(2,1)S(1)}, bf16[192,2048]{1,0:T(8,128)(2,1)}, u32[]{:S(2)}, u32[]{:S(2)}) collective-permute-start(bf16[192,2048]{1,0:T(8,128)(2,1)S(1)} %bitcast_add_fusion.5), channel_id=1, source_target_pairs={{0,32},{1,225},{2,34},{3,227},{4,36},{5,229},{6,38},{7,231},{8,40}... | collective-permute-start | bytes 2359304 | tf_op jit(solution)/shard_map/ppermute | solution.py:323
  216.4 14.7 %collective-permute-start.10 = (bf16[192,2048]{1,0:T(8,128)(2,1)}, bf16[192,2048]{1,0:T(8,128)(2,1)}, u32[]{:S(2)}, u32[]{:S(2)}) collective-permute-start(bf16[192,2048]{1,0:T(8,128)(2,1)} %bitcast_add_fusion.4), channel_id=1, source_target_pairs={{0,32},{1,225},{2,34},{3,227},{4,36},{5,229},{6,38},{7,231},{8,40}... | collective-permute-start | bytes 2359304 | tf_op jit(solution)/shard_map/ppermute | solution.py:323
  225.1 14.5 %collective-permute-start.9 = (bf16[192,2048]{1,0:T(8,128)(2,1)}, bf16[192,2048]{1,0:T(8,128)(2,1)}, u32[]{:S(2)}, u32[]{:S(2)}) collective-permute-start(bf16[192,2048]{1,0:T(8,128)(2,1)} %bitcast_add_fusion.3), channel_id=1, source_target_pairs={{0,32},{1,225},{2,34},{3,227},{4,36},{5,229},{6,38},{7,231},{8,40}... | collective-permute-start | bytes 2359304 | tf_op jit(solution)/shard_map/ppermute | solution.py:323
  241.1 13.3 %collective-permute-start.11 = (bf16[192,2048]{1,0:T(8,128)(2,1)S(1)}, bf16[192,2048]{1,0:T(8,128)(2,1)S(1)}, u32[]{:S(2)}, u32[]{:S(2)}) collective-permute-start(bf16[192,2048]{1,0:T(8,128)(2,1)S(1)} %bitcast_add_fusion.1), channel_id=1, source_target_pairs={{0,32},{1,225},{2,34},{3,227},{4,36},{5,229},{6,38},{7,231},{8,40}... | collective-permute-start | bytes 2359304 | tf_op jit(solution)/shard_map/ppermute | solution.py:323
  241.1 21.6 %collective-permute-start.13 = (bf16[192,2048]{1,0:T(8,128)(2,1)S(1)}, bf16[192,2048]{1,0:T(8,128)(2,1)S(1)}, u32[]{:S(2)}, u32[]{:S(2)}) collective-permute-start(bf16[192,2048]{1,0:T(8,128)(2,1)S(1)} %bitcast_add_fusion.2), channel_id=1, source_target_pairs={{0,32},{1,225},{2,34},{3,227},{4,36},{5,229},{6,38},{7,231},{8,40}... | collective-permute-start | bytes 2359304 | tf_op jit(solution)/shard_map/ppermute | solution.py:323
  255.6 15.6 %collective-permute-start.12 = (bf16[192,2048]{1,0:T(8,128)(2,1)S(1)}, bf16[192,2048]{1,0:T(8,128)(2,1)S(1)}, u32[]{:S(2)}, u32[]{:S(2)}) collective-permute-start(bf16[192,2048]{1,0:T(8,128)(2,1)S(1)} %bitcast_add_fusion), channel_id=1, source_target_pairs={{0,32},{1,225},{2,34},{3,227},{4,36},{5,229},{6,38},{7,231},{8,40}... | collective-permute-start | bytes 2359304 | tf_op jit(solution)/shard_map/ppermute | solution.py:323
  262.8 0.9 copy-start
  271.2 0.9 copy-start.1
Sparse Core Ops, SparseCore 0:
  10.8 152.9 all-gather.2

commit v4 on v3

--- a/solution.py
+++ b/solution.py
@@ -283,14 +283,14 @@
     groups, rows, width = rest.shape
     return pl.pallas_call(
         final_kernel,
-        grid=(width // WIDE,),
+        grid=(1,),
         in_specs=[
             pl.BlockSpec(memory_space=pltpu.SMEM),
-            pl.BlockSpec((1, rows, WIDE), lambda i: (groups - 1, 0, i)),
-            pl.BlockSpec((rows, WIDE), lambda i: (0, i)),
+            pl.BlockSpec((1, rows, width), lambda i: (groups - 1, 0, 0)),
+            pl.BlockSpec((rows, width), lambda i: (0, 0)),
         ]
         + [pl.BlockSpec(memory_space=pl.ANY)] * len(done),
-        out_specs=pl.BlockSpec((shape[0], 2, WIDE), lambda i: (0, 0, at + i)),
+        out_specs=pl.BlockSpec((shape[0], 2, width), lambda i: (0, 0, at)),
         out_shape=jax.ShapeDtypeStruct(shape, F32),
         input_output_aliases={3 + k: k for k in range(len(done))},
         compiler_params=PARAMS,
@@ -361,15 +361,15 @@
     for turn in range(1, groups - 1):
         if rings[0].turn < groups - 2:
             rings[0].step()
+        rings[1].step()
         if turn in (1, 2, 4, 5):
             hidden_piece((turn - 1) % 3, turn // 3)
         else:
             grads = gate_piece(turn // 3 - 1, grads)
-        rings[1].step()
     out_shape, grad_down = (units, local, width), ()
     for half in range(2):
         got = clock(rings[half].got)
-        grad_down = (final(clock.value, got, rings[half].rest, out_shape, 2 * half, grad_down),)
+        grad_down = (final(clock.value, got, rings[half].rest, out_shape, half, grad_down),)
     return (grads[0], grads[1], grad_down[0])
 
 

time: 282 us -> 283 us (level)
  waiting for transfers between devices: 140 us -> 143 us
  transfers between devices with their start and end apart: 17 -> 17, of which waited for: 14 -> 15; matrix products, arithmetic and copies ran while one was open for 7% -> 7% of each run, Pallas kernels for 28% -> 28%
where the time goes in v4:
time: 283 us; the launch traced here: 282 us
  waiting for transfers between devices  143 us (51%)
  Pallas kernels  82.7 us (29%)
  other arithmetic  19.8 us (7%)
  starting transfers between devices  17.4 us (6%)
  between operations  14.2 us (5%)
  local copies, waits for them, and re-layouts  5.24 us (2%)
    ppermute x14, waiting for transfers between devices, send(): self.got = lax.ppermute(blocks, ('dp', 'expert'), self.pairs)  86.4 us
    all_to_all x2, waiting for transfers between devices, exchange(): lax.all_to_all(rows, 'expert', split_axis=0, concat_axis=0, tiled=True)  56.2 us
    pallas_call x4, Pallas kernels, hidden_grad(): pl.pallas_call(functools.partial(hidden_grad_kernel, count), grid=(each *...  25.4 us
    pallas_call x2, Pallas kernels, partial_down(): pl.pallas_call(down_kernel, grid=(count, 2), in_specs=[pl.BlockSpec(memor...  24.6 us
    add x12, other arithmetic, step(): self.send(self.clock(self.clock(self.got) + self.rest[self.turn]))  19.2 us
    all_to_all x2, starting transfers between devices, exchange(): lax.all_to_all(rows, 'expert', split_axis=0, concat_axis=0, tiled=True)  12.2 us
    pallas_call x2, Pallas kernels, dispatch(): pl.pallas_call(dispatch_kernel, grid=(count,), in_specs=[pl.BlockSpec(ids...  10.2 us
    pallas_call x2, Pallas kernels, gate_grads(): pl.pallas_call(functools.partial(gate_grads_kernel, sources), grid=(1,),...  9.17 us
  transfers between devices with their start and end apart: 17, of which 15 were waited for; matrix products, arithmetic and copies ran while one was open for 7% of the time, Pallas kernels for 28%

profile of v4, /device:TPU:8, one launch (start us, length us, event | category | flops | bytes accessed | tf_op | source)
XLA Modules:
  0.0 281.9 jit_solution(5299880481798964053)
XLA Ops:
  7.2 3.4 %copy.15 = bf16[96,2,4096]{2,0,1:T(8,128)(2,1)} copy(bf16[96,2,4096]{2,1,0:T(2,128)(2,1)} %param.11) | data formatting | bytes 3145728 | tf_op args[5]
  10.7 5.1 %dispatch.3 = bf16[32,544,128]{2,1,0:T(8,128)(2,1)} custom-call(s32[8,128]{1,0:T(8,128)} %bitcast.39, bf16[8,128]{1,0:T(8,128)(2,1)} %bitcast.41, bf16[128,4096]{1,0:T(8,128)(2,1)} %grad_ref.3), custom_call_target="tpu_custom_call" | custom-call | flops 570425344 | bytes 6291456 | tf_op jit(solution)/shard_map/dispatch/pallas_call | solution.py:69
  15.8 7.6 %all-to-all-start.1 = ((bf16[32,544,128]{2,1,0:T(8,128)(2,1)}), bf16[32,544,128]{2,1,0:T(8,128)(2,1)}, u32[]{:S(2)}, u32[]{:S(2)}) async-start(bf16[32,544,128]{2,1,0:T(8,128)(2,1)} %dispatch.3), calls=%async_computation.1 | async-start | bytes 8912896 | tf_op jit(solution)/shard_map/all_to_all | solution.py:338
  23.4 7.5 %arrange.1 = (bf16[2,768,544]{2,1,0:T(8,128)(2,1)}, bf16[2,544,768]{2,1,0:T(8,128)(2,1)}, bf16[2,544,768]{2,1,0:T(8,128)(2,1)}) custom-call(bf16[2,544,768]{2,1,0:T(8,128)(2,1)} %gate_ref.1, bf16[2,544,768]{2,1,0:T(8,128)(2,1)} %up_ref.1), custom_call_target="tpu_custom_call" | custom-call | flops 2727346176 | bytes 9437184 | tf_op jit(solution)/shard_map/arrange/pallas_call | solution.py:113
  30.9 5.0 %dispatch.2 = bf16[32,544,128]{2,1,0:T(8,128)(2,1)} custom-call(s32[8,128]{1,0:T(8,128)} %bitcast.40, bf16[8,128]{1,0:T(8,128)(2,1)} %bitcast.42, bf16[128,4096]{1,0:T(8,128)(2,1)} %grad_ref.3, bf16[2,768,544]{2,1,0:T(8,128)(2,1)} %get-tuple-element.90.refs_0_.hidden_ref), custom_call_target="tpu_custom_call" | custom-call | flops 570425344 | bytes 6291456 | tf_op jit(solution)/shard_map/dispatch/pallas_call | solution.py:69
  35.9 46.4 %all-to-all-done.1.rows_ref = bf16[32,544,128]{2,1,0:T(8,128)(2,1)} async-done(((bf16[32,544,128]{2,1,0:T(8,128)(2,1)}), bf16[32,544,128]{2,1,0:T(8,128)(2,1)}, u32[]{:S(2)}, u32[]{:S(2)}) %all-to-all-start.1) | async-done | bytes 4456480 | tf_op jit(solution)/shard_map/all_to_all | solution.py:338
  82.3 4.7 %all-to-all-start = ((bf16[32,544,128]{2,1,0:T(8,128)(2,1)}), bf16[32,544,128]{2,1,0:T(8,128)(2,1)}, u32[]{:S(2)}, u32[]{:S(2)}) async-start(bf16[32,544,128]{2,1,0:T(8,128)(2,1)} %dispatch.2), calls=%async_computation | async-start | bytes 8912896 | tf_op jit(solution)/shard_map/all_to_all | solution.py:338
  87.0 0.6 pad_add_fusion.place_ref.refs_0_.after_ref
  87.5 12.3 %partial_down.2 = (bf16[2,544,2048]{2,1,0:T(8,128)(2,1)}, bf16[8,192,2048]{2,1,0:T(8,128)(2,1)}, bf16[192,2048]{1,0:T(8,128)(2,1)}) custom-call(s32[2]{0:T(128)} %pad_add_fusion.place_ref.refs_0_.after_ref, bf16[32,544,128]{2,1,0:T(8,128)(2,1)} %all-to-all-done.1.rows_ref, bf16[2,768,544]{2,1,0:T(8,128)(2,1)} %get-tuple-element.90.refs_0_.hidden_ref), custom_call_target="tpu_custom_call" | custom-call | flops 3422552064 | bytes 18874368 | tf_op jit(solution)/shard_map/partial_down/pallas_call | solution.py:164
  99.9 1.9 collective-permute-start
  101.8 31.0 %collective-permute-done = bf16[192,2048]{1,0:T(8,128)(2,1)S(1)} collective-permute-done((bf16[192,2048]{1,0:T(8,128)(2,1)}, bf16[192,2048]{1,0:T(8,128)(2,1)S(1)}, u32[]{:S(2)}, u32[]{:S(2)}) %collective-permute-start) | collective-permute-done | bytes 786464 | tf_op jit(solution)/shard_map/ppermute | solution.py:323
  132.8 1.2 bitcast_add_fusion.11
  134.1 9.8 %all-to-all-done.rows_ref = bf16[32,544,128]{2,1,0:T(8,128)(2,1)} async-done(((bf16[32,544,128]{2,1,0:T(8,128)(2,1)}), bf16[32,544,128]{2,1,0:T(8,128)(2,1)}, u32[]{:S(2)}, u32[]{:S(2)}) %all-to-all-start) | async-done | bytes 4456480 | tf_op jit(solution)/shard_map/all_to_all | solution.py:338
  143.9 12.2 %partial_down.3 = (bf16[2,544,2048]{2,1,0:T(8,128)(2,1)}, bf16[8,192,2048]{2,1,0:T(8,128)(2,1)}, bf16[192,2048]{1,0:T(8,128)(2,1)}) custom-call(s32[2]{0:T(128)} %pad_add_fusion.place_ref.refs_0_.after_ref, bf16[32,544,128]{2,1,0:T(8,128)(2,1)} %all-to-all-done.rows_ref, bf16[2,768,544]{2,1,0:T(8,128)(2,1)} %get-tuple-element.90.refs_0_.hidden_ref), custom_call_target="tpu_custom_call" | custom-call | flops 3422552064 | bytes 18874368 | tf_op jit(solution)/shard_map/partial_down/pallas_call | solution.py:164
  156.1 1.9 collective-permute-start.1
  158.0 5.4 %collective-permute-done.2 = bf16[192,2048]{1,0:T(8,128)(2,1)S(1)} collective-permute-done((bf16[192,2048]{1,0:T(8,128)(2,1)S(1)}, bf16[192,2048]{1,0:T(8,128)(2,1)S(1)}, u32[]{:S(2)}, u32[]{:S(2)}) %collective-permute-start.2) | collective-permute-done | bytes 786464 | tf_op jit(solution)/shard_map/ppermute | solution.py:323
  163.4 1.2 bitcast_add_fusion.10
  164.7 7.4 %collective-permute-done.1 = bf16[192,2048]{1,0:T(8,128)(2,1)S(1)} collective-permute-done((bf16[192,2048]{1,0:T(8,128)(2,1)}, bf16[192,2048]{1,0:T(8,128)(2,1)S(1)}, u32[]{:S(2)}, u32[]{:S(2)}) %collective-permute-start.1) | collective-permute-done | bytes 786464 | tf_op jit(solution)/shard_map/ppermute | solution.py:323
  172.1 2.2 bitcast_add_fusion.9
  174.4 6.2 %hidden_grad.4.refs_2_ = f32[544,768]{1,0:T(8,128)} custom-call(s32[2]{0:T(128)} %pad_add_fusion.place_ref.refs_0_.after_ref, bf16[2,544,2048]{2,1,0:T(8,128)(2,1)} %get-tuple-element.115.refs_1_, bf16[8,2,96,4096]{3,2,1,0:T(8,128)(2,1)} %bitcast.32), custom_call_target="tpu_custom_call" | custom-call | flops 1711276032 | bytes 9437184 | tf_op jit(solution)/shard_map/hidden_grad/pallas_call | solution.py:221
  180.6 0.1 collective-permute-done.4
  180.7 1.2 bitcast_add_fusion.8
  182.0 7.1 %collective-permute-done.3 = bf16[192,2048]{1,0:T(8,128)(2,1)} collective-permute-done((bf16[192,2048]{1,0:T(8,128)(2,1)}, bf16[192,2048]{1,0:T(8,128)(2,1)}, u32[]{:S(2)}, u32[]{:S(2)}) %collective-permute-start.3) | collective-permute-done | bytes 786464 | tf_op jit(solution)/shard_map/ppermute | solution.py:323
  189.1 2.3 bitcast_add_fusion.7
  191.4 6.6 %hidden_grad.5.total_ref = f32[544,768]{1,0:T(8,128)} custom-call(s32[2]{0:T(128)} %pad_add_fusion.place_ref.refs_0_.after_ref, bf16[2,544,2048]{2,1,0:T(8,128)(2,1)} %get-tuple-element.125.refs_1_, f32[544,768]{1,0:T(8,128)} %hidden_grad.4.refs_2_, bf16[8,2,96,4096]{3,2,1,0:T(8,128)(2,1)} %bitcast.33), custom_call_target="tpu_custom_call" | custom-call | flops 1711276032 | bytes 9437184 | tf_op jit(solution)/shard_map/hidden_grad/pallas_call | solution.py:221
  198.1 1.2 bitcast_add_fusion.6
  199.4 6.6 %collective-permute-done.5 = bf16[192,2048]{1,0:T(8,128)(2,1)} collective-permute-done((bf16[192,2048]{1,0:T(8,128)(2,1)}, bf16[192,2048]{1,0:T(8,128)(2,1)}, u32[]{:S(2)}, u32[]{:S(2)}) %collective-permute-start.5) | collective-permute-done | bytes 786464 | tf_op jit(solution)/shard_map/ppermute | solution.py:323
  206.0 2.3 bitcast_add_fusion.5
  208.3 4.6 %gate_grads.2 = (bf16[2,544,768]{2,1,0:T(8,128)(2,1)}, bf16[2,544,768]{2,1,0:T(8,128)(2,1)}) custom-call(s32[2]{0:T(128)} %pad_add_fusion.place_ref.refs_0_.after_ref, f32[544,768]{1,0:T(8,128)} %hidden_grad.5.total_ref, bf16[2,544,768]{2,1,0:T(8,128)(2,1)} %get-tuple-element.137.gate_ref, bf16[2,544,768]{2,1,0:T(8,128)(2,1)} %get-tuple-element.138.up_ref), custom_call_target="tpu_custom_call" | custom-call | flops 909115392 | bytes 5242880 | tf_op jit(solution)/shard_map/gate_grads/pallas_call | solution.py:255
  212.9 1.5 collective-permute-done.8
  214.4 1.2 bitcast_add_fusion.4
  215.7 7.1 %collective-permute-done.7 = bf16[192,2048]{1,0:T(8,128)(2,1)} collective-permute-done((bf16[192,2048]{1,0:T(8,128)(2,1)}, bf16[192,2048]{1,0:T(8,128)(2,1)}, u32[]{:S(2)}, u32[]{:S(2)}) %collective-permute-start.7) | collective-permute-done | bytes 786464 | tf_op jit(solution)/shard_map/ppermute | solution.py:323
  222.8 2.3 bitcast_add_fusion.3
  225.2 6.0 %hidden_grad.6.refs_2_ = f32[544,768]{1,0:T(8,128)} custom-call(s32[2]{0:T(128)} %pad_add_fusion.place_ref.refs_0_.after_ref, bf16[2,544,2048]{2,1,0:T(8,128)(2,1)} %get-tuple-element.115.refs_1_, bf16[8,2,96,4096]{3,2,1,0:T(8,128)(2,1)} %bitcast.34), custom_call_target="tpu_custom_call" | custom-call | flops 1711276032 | bytes 9437184 | tf_op jit(solution)/shard_map/hidden_grad/pallas_call | solution.py:221
  231.2 1.2 bitcast_add_fusion.2
  232.5 7.2 %collective-permute-done.9 = bf16[192,2048]{1,0:T(8,128)(2,1)} collective-permute-done((bf16[192,2048]{1,0:T(8,128)(2,1)}, bf16[192,2048]{1,0:T(8,128)(2,1)}, u32[]{:S(2)}, u32[]{:S(2)}) %collective-permute-start.9) | collective-permute-done | bytes 786464 | tf_op jit(solution)/shard_map/ppermute | solution.py:323
  239.7 1.5 bitcast_add_fusion.1
  241.2 6.6 %hidden_grad.7.total_ref = f32[544,768]{1,0:T(8,128)} custom-call(s32[2]{0:T(128)} %pad_add_fusion.place_ref.refs_0_.after_ref, bf16[2,544,2048]{2,1,0:T(8,128)(2,1)} %get-tuple-element.125.refs_1_, f32[544,768]{1,0:T(8,128)} %hidden_grad.6.refs_2_, bf16[8,2,96,4096]{3,2,1,0:T(8,128)(2,1)} %bitcast.35), custom_call_target="tpu_custom_call" | custom-call | flops 1711276032 | bytes 9437184 | tf_op jit(solution)/shard_map/hidden_grad/pallas_call | solution.py:221
  247.8 0.8 collective-permute-start.13
  248.6 5.8 %collective-permute-done.11 = bf16[192,2048]{1,0:T(8,128)(2,1)S(1)} collective-permute-done((bf16[192,2048]{1,0:T(8,128)(2,1)S(1)}, bf16[192,2048]{1,0:T(8,128)(2,1)S(1)}, u32[]{:S(2)}, u32[]{:S(2)}) %collective-permute-start.11) | collective-permute-done | bytes 786464 | tf_op jit(solution)/shard_map/ppermute | solution.py:323
  254.4 1.2 bitcast_add_fusion
  255.7 4.6 %gate_grads.3 = (bf16[2,544,768]{2,1,0:T(8,128)(2,1)}, bf16[2,544,768]{2,1,0:T(8,128)(2,1)}) custom-call(s32[2]{0:T(128)} %pad_add_fusion.place_ref.refs_0_.after_ref, f32[544,768]{1,0:T(8,128)} %hidden_grad.7.total_ref, bf16[2,544,768]{2,1,0:T(8,128)(2,1)} %get-tuple-element.137.gate_ref, ...), custom_call_target="tpu_custom_call", output_to_operand_aliasing={{0}: (4, {}), {1}: (5, {})} | custom-call | flops 909115392 | bytes 5242880 | tf_op jit(solution)/shard_map/gate_grads/pallas_call | solution.py:255
  260.3 2.5 collective-permute-done.13.arrived_ref
  262.8 0.9 copy-done
  263.7 2.9 %final.2.refs_0_ = f32[96,2,4096]{2,1,0:T(2,128)} custom-call(s32[2]{0:T(128)} %pad_add_fusion.place_ref.refs_0_.after_ref, bf16[8,192,2048]{2,1,0:T(8,128)(2,1)} %get-tuple-element.97.own_ref, bf16[192,2048]{1,0:T(8,128)(2,1)} %copy-done), custom_call_target="tpu_custom_call" | custom-call | flops 393216 | bytes 3145728 | tf_op jit(solution)/shard_map/final/pallas_call | solution.py:284
  266.7 4.6 %collective-permute-done.12.arrived_ref = bf16[192,2048]{1,0:T(8,128)(2,1)S(1)} collective-permute-done((bf16[192,2048]{1,0:T(8,128)(2,1)S(1)}, bf16[192,2048]{1,0:T(8,128)(2,1)S(1)}, u32[]{:S(2)}, u32[]{:S(2)}) %collective-permute-start.12) | collective-permute-done | bytes 786464 | tf_op jit(solution)/shard_map/ppermute | solution.py:323
  271.3 0.9 copy-done.1
  272.2 2.9 %final.3 = f32[96,2,4096]{2,1,0:T(2,128)} custom-call(s32[2]{0:T(128)} %pad_add_fusion.place_ref.refs_0_.after_ref, bf16[8,192,2048]{2,1,0:T(8,128)(2,1)} %get-tuple-element.110.own_ref, bf16[192,2048]{1,0:T(8,128)(2,1)} %copy-done.1, f32[96,2,4096]{2,1,0:T(2,128)} %final.2.refs_0_), custom_call_target="tpu_custom_call", output_to_operand_aliasing={{}: (3, {})} | custom-call | flops 393216 | bytes 3145728 | tf_op jit(solution)/shard_map/final/pallas_call | solution.py:284
  (23 shorter events, 0.7 us)
Async XLA Ops:
  7.2 167.2 %all-gather.3.cloned.1.call-start = ((), (), s32[]{:S(2)}) async-start(), calls=%async_computation.2 | async-start | bytes 14155776 | tf_op jit(solution)/shard_map/all_gather | solution.py:340
  15.8 66.5 %all-to-all-start.1 = ((bf16[32,544,128]{2,1,0:T(8,128)(2,1)}), bf16[32,544,128]{2,1,0:T(8,128)(2,1)}, u32[]{:S(2)}, u32[]{:S(2)}) async-start(bf16[32,544,128]{2,1,0:T(8,128)(2,1)} %dispatch.3), calls=%async_computation.1 | async-start | bytes 8912896 | tf_op jit(solution)/shard_map/all_to_all | solution.py:338
  82.3 61.6 %all-to-all-start = ((bf16[32,544,128]{2,1,0:T(8,128)(2,1)}), bf16[32,544,128]{2,1,0:T(8,128)(2,1)}, u32[]{:S(2)}, u32[]{:S(2)}) async-start(bf16[32,544,128]{2,1,0:T(8,128)(2,1)} %dispatch.2), calls=%async_computation | async-start | bytes 8912896 | tf_op jit(solution)/shard_map/all_to_all | solution.py:338
  99.9 32.9 %collective-permute-start = (bf16[192,2048]{1,0:T(8,128)(2,1)}, bf16[192,2048]{1,0:T(8,128)(2,1)S(1)}, u32[]{:S(2)}, u32[]{:S(2)}) collective-permute-start(bf16[192,2048]{1,0:T(8,128)(2,1)} %get-tuple-element.94), channel_id=1, source_target_pairs={{0,32},{1,225},{2,34},{3,227},{4,36},{5,229},{6,38},{7,231},{8,40}... | collective-permute-start | bytes 2359304 | tf_op jit(solution)/shard_map/ppermute | solution.py:323
  134.0 29.4 %collective-permute-start.2 = (bf16[192,2048]{1,0:T(8,128)(2,1)S(1)}, bf16[192,2048]{1,0:T(8,128)(2,1)S(1)}, u32[]{:S(2)}, u32[]{:S(2)}) collective-permute-start(bf16[192,2048]{1,0:T(8,128)(2,1)S(1)} %bitcast_add_fusion.11), channel_id=1, source_target_pairs={{0,32},{1,225},{2,34},{3,227},{4,36},{5,229},{6,38},{7,231},{8,40}... | collective-permute-start | bytes 2359304 | tf_op jit(solution)/shard_map/ppermute | solution.py:323
  156.1 16.0 %collective-permute-start.1 = (bf16[192,2048]{1,0:T(8,128)(2,1)}, bf16[192,2048]{1,0:T(8,128)(2,1)S(1)}, u32[]{:S(2)}, u32[]{:S(2)}) collective-permute-start(bf16[192,2048]{1,0:T(8,128)(2,1)} %get-tuple-element.103), channel_id=1, source_target_pairs={{0,32},{1,225},{2,34},{3,227},{4,36},{5,229},{6,38},{7,231},{8,40}... | collective-permute-start | bytes 2359304 | tf_op jit(solution)/shard_map/ppermute | solution.py:323
  164.6 16.1 %collective-permute-start.4 = (bf16[192,2048]{1,0:T(8,128)(2,1)S(1)}, bf16[192,2048]{1,0:T(8,128)(2,1)}, u32[]{:S(2)}, u32[]{:S(2)}) collective-permute-start(bf16[192,2048]{1,0:T(8,128)(2,1)S(1)} %bitcast_add_fusion.10), channel_id=1, source_target_pairs={{0,32},{1,225},{2,34},{3,227},{4,36},{5,229},{6,38},{7,231},{8,40}... | collective-permute-start | bytes 2359304 | tf_op jit(solution)/shard_map/ppermute | solution.py:323
  172.1 8.5 %slice-start = ((s8[6291456]{0:T(1024)(128)(4,1)}), s8[2097152]{0:T(1024)(128)(4,1)S(1)}, s32[]{:S(2)}) async-start(s8[6291456]{0:T(1024)(128)(4,1)} %bitcast.36), calls=%async_computation.3 | async-start | bytes 4194304
  174.4 14.7 %collective-permute-start.3 = (bf16[192,2048]{1,0:T(8,128)(2,1)}, bf16[192,2048]{1,0:T(8,128)(2,1)}, u32[]{:S(2)}, u32[]{:S(2)}) collective-permute-start(bf16[192,2048]{1,0:T(8,128)(2,1)} %bitcast_add_fusion.9), channel_id=1, source_target_pairs={{0,32},{1,225},{2,34},{3,227},{4,36},{5,229},{6,38},{7,231},{8,40}... | collective-permute-start | bytes 2359304 | tf_op jit(solution)/shard_map/ppermute | solution.py:323
  174.4 6.3 %slice-start.1 = ((s8[6291456]{0:T(1024)(128)(4,1)}), s8[4194304]{0:T(1024)(128)(4,1)S(1)}, s32[]{:S(2)}) async-start(s8[6291456]{0:T(1024)(128)(4,1)} %bitcast.36), calls=%async_computation.4 | async-start | bytes 8388608
  181.9 16.1 %collective-permute-start.6 = (bf16[192,2048]{1,0:T(8,128)(2,1)S(1)}, bf16[192,2048]{1,0:T(8,128)(2,1)}, u32[]{:S(2)}, u32[]{:S(2)}) collective-permute-start(bf16[192,2048]{1,0:T(8,128)(2,1)S(1)} %bitcast_add_fusion.8), channel_id=1, source_target_pairs={{0,32},{1,225},{2,34},{3,227},{4,36},{5,229},{6,38},{7,231},{8,40}... | collective-permute-start | bytes 2359304 | tf_op jit(solution)/shard_map/ppermute | solution.py:323
  191.4 14.5 %collective-permute-start.5 = (bf16[192,2048]{1,0:T(8,128)(2,1)}, bf16[192,2048]{1,0:T(8,128)(2,1)}, u32[]{:S(2)}, u32[]{:S(2)}) collective-permute-start(bf16[192,2048]{1,0:T(8,128)(2,1)} %bitcast_add_fusion.7), channel_id=1, source_target_pairs={{0,32},{1,225},{2,34},{3,227},{4,36},{5,229},{6,38},{7,231},{8,40}... | collective-permute-start | bytes 2359304 | tf_op jit(solution)/shard_map/ppermute | solution.py:323
  199.3 15.1 %collective-permute-start.8 = (bf16[192,2048]{1,0:T(8,128)(2,1)S(1)}, bf16[192,2048]{1,0:T(8,128)(2,1)}, u32[]{:S(2)}, u32[]{:S(2)}) collective-permute-start(bf16[192,2048]{1,0:T(8,128)(2,1)S(1)} %bitcast_add_fusion.6), channel_id=1, source_target_pairs={{0,32},{1,225},{2,34},{3,227},{4,36},{5,229},{6,38},{7,231},{8,40}... | collective-permute-start | bytes 2359304 | tf_op jit(solution)/shard_map/ppermute | solution.py:323
  208.3 14.5 %collective-permute-start.7 = (bf16[192,2048]{1,0:T(8,128)(2,1)}, bf16[192,2048]{1,0:T(8,128)(2,1)}, u32[]{:S(2)}, u32[]{:S(2)}) collective-permute-start(bf16[192,2048]{1,0:T(8,128)(2,1)} %bitcast_add_fusion.5), channel_id=1, source_target_pairs={{0,32},{1,225},{2,34},{3,227},{4,36},{5,229},{6,38},{7,231},{8,40}... | collective-permute-start | bytes 2359304 | tf_op jit(solution)/shard_map/ppermute | solution.py:323
  215.6 15.6 %collective-permute-start.10 = (bf16[192,2048]{1,0:T(8,128)(2,1)S(1)}, bf16[192,2048]{1,0:T(8,128)(2,1)}, u32[]{:S(2)}, u32[]{:S(2)}) collective-permute-start(bf16[192,2048]{1,0:T(8,128)(2,1)S(1)} %bitcast_add_fusion.4), channel_id=1, source_target_pairs={{0,32},{1,225},{2,34},{3,227},{4,36},{5,229},{6,38},{7,231},{8,40}... | collective-permute-start | bytes 2359304 | tf_op jit(solution)/shard_map/ppermute | solution.py:323
  225.2 14.5 %collective-permute-start.9 = (bf16[192,2048]{1,0:T(8,128)(2,1)}, bf16[192,2048]{1,0:T(8,128)(2,1)}, u32[]{:S(2)}, u32[]{:S(2)}) collective-permute-start(bf16[192,2048]{1,0:T(8,128)(2,1)} %bitcast_add_fusion.3), channel_id=1, source_target_pairs={{0,32},{1,225},{2,34},{3,227},{4,36},{5,229},{6,38},{7,231},{8,40}... | collective-permute-start | bytes 2359304 | tf_op jit(solution)/shard_map/ppermute | solution.py:323
  241.1 13.3 %collective-permute-start.11 = (bf16[192,2048]{1,0:T(8,128)(2,1)S(1)}, bf16[192,2048]{1,0:T(8,128)(2,1)S(1)}, u32[]{:S(2)}, u32[]{:S(2)}) collective-permute-start(bf16[192,2048]{1,0:T(8,128)(2,1)S(1)} %bitcast_add_fusion.1), channel_id=1, source_target_pairs={{0,32},{1,225},{2,34},{3,227},{4,36},{5,229},{6,38},{7,231},{8,40}... | collective-permute-start | bytes 2359304 | tf_op jit(solution)/shard_map/ppermute | solution.py:323
  247.8 15.0 %collective-permute-start.13 = (bf16[192,2048]{1,0:T(8,128)(2,1)S(1)}, bf16[192,2048]{1,0:T(8,128)(2,1)S(1)}, u32[]{:S(2)}, u32[]{:S(2)}) collective-permute-start(bf16[192,2048]{1,0:T(8,128)(2,1)S(1)} %bitcast_add_fusion.2), channel_id=1, source_target_pairs={{0,32},{1,225},{2,34},{3,227},{4,36},{5,229},{6,38},{7,231},{8,40}... | collective-permute-start | bytes 2359304 | tf_op jit(solution)/shard_map/ppermute | solution.py:323
  255.6 15.6 %collective-permute-start.12 = (bf16[192,2048]{1,0:T(8,128)(2,1)S(1)}, bf16[192,2048]{1,0:T(8,128)(2,1)S(1)}, u32[]{:S(2)}, u32[]{:S(2)}) collective-permute-start(bf16[192,2048]{1,0:T(8,128)(2,1)S(1)} %bitcast_add_fusion), channel_id=1, source_target_pairs={{0,32},{1,225},{2,34},{3,227},{4,36},{5,229},{6,38},{7,231},{8,40}... | collective-permute-start | bytes 2359304 | tf_op jit(solution)/shard_map/ppermute | solution.py:323
  262.8 0.9 copy-start
  271.3 0.9 copy-start.1
Sparse Core Ops, SparseCore 0:
  10.8 152.9 all-gather.2
